TPU v7x, 128 devices: a whole 4x4x4 slice. The times are simulated.
128 devices in a mesh: dp: 16 (over x, z_lo, core), expert: 8 (over y, z_hi).
Axes of the slice: x: 4, y: 4, z: 4 (z_hi: 2, z_lo: 2; z = z_hi * 2 + z_lo), core: 2. Of those that a mesh axis runs over, the one named last changes fastest.
Arguments:
- tokens: bfloat16 [1024, 7168], P(('dp', 'expert')), may hold values from -6 to 6
- assign: int32 [1024, 1], P(('dp', 'expert')), may hold values from 0 to 7; in each aligned block of 8 rows (0 to 7, 8 to 15, ...) at most 2 rows name the same one
- copy_share: int32 [128, 8], P(('dp', 'expert')), may hold values from 0 to 2
- copy_plan: int32 [8], replicated, may hold values from 0 to 7, as said below
- grad_out: bfloat16 [1024, 7168], P(('dp', 'expert')), may hold values from -6 to 6
- w_gate: bfloat16 [8, 7168, 2048], P('expert', None, 'dp'), may hold values from -0.0625 to 0.0625
- w_up: bfloat16 [8, 7168, 2048], P('expert', None, 'dp'), may hold values from -0.0625 to 0.0625
- w_down: bfloat16 [8, 2048, 7168], P('expert', 'dp'), may hold values from -0.125 to 0.125
Outputs:
- mixed: bfloat16 [1024, 7168], P(('dp', 'expert'))
- grad_in: bfloat16 [1024, 7168], P(('dp', 'expert'))
- grad_gate_w: bfloat16 [8, 7168, 2048], P('expert', None, 'dp')
- grad_up_w: bfloat16 [8, 7168, 2048], P('expert', None, 'dp')
- grad_down_w: bfloat16 [8, 2048, 7168], P('expert', 'dp')
- copy_grad_gate: bfloat16 [8, 7168, 2048], P('expert', None, 'dp')
- copy_grad_up: bfloat16 [8, 7168, 2048], P('expert', None, 'dp')
- copy_grad_down: bfloat16 [8, 2048, 7168], P('expert', 'dp')
Inputs may be any that keep to these rules, and one draw needn't show every extreme that they name: `assign`: among the rows of one device no expert is named more than 2 times. `copy_plan`: each expert number appears exactly once.
All inputs are finite; a program needn't handle non-finite values.
Results may differ from a plain program's by a relative error of at most 0.0051.
Values may be sent and summed in bfloat16 or wider, within the bound.
A program may use at most 192 MiB of HBM per device.

v0:
```python
import jax
import jax.numpy as jnp
from jax import lax
from jax.sharding import PartitionSpec as P


def slot_matrix(assign, copy_share, copy_plan, experts, capacity):
    expert_of = assign[:, 0]
    numbers = jnp.arange(experts, dtype=jnp.int32)
    onehot = (expert_of[:, None] == numbers[None, :]).astype(jnp.int32)
    before = jnp.cumsum(onehot, axis=0) - onehot
    rank_in = jnp.sum(before * onehot, axis=1)
    limit_rows = jnp.sum(copy_share[0][None, :] * onehot, axis=1)
    holder = jnp.sum(
        numbers[None, :] * (copy_plan[None, :] == expert_of[:, None]).astype(jnp.int32), axis=1
    )
    owned = experts * capacity
    target = jnp.where(
        rank_in < limit_rows, owned + holder * capacity + rank_in, expert_of * capacity + rank_in
    )
    places = jnp.arange(2 * owned, dtype=jnp.int32)
    return (places[:, None] == target[None, :]).astype(jnp.bfloat16)


def copy_weights(gate_w, up_w, down_w, copy_plan, experts):
    stacked = jnp.stack([gate_w, up_w, down_w.T])
    width = stacked.shape[1]
    units = stacked.shape[2]
    spread = lax.all_to_all(stacked, "expert", split_axis=1, concat_axis=1, tiled=True)
    pieces = spread.reshape(3, experts, width // experts, units)
    chosen = jnp.take(pieces, copy_plan, axis=1).reshape(3, width, units)
    collected = lax.all_to_all(chosen, "expert", split_axis=1, concat_axis=1, tiled=True)
    return (collected[0], collected[1], collected[2].T)


def contract_rows(left, right):
    return lax.dot_general(
        left, right, (((0,), (0,)), ((), ())), preferred_element_type=jnp.float32
    )


def body(tokens, assign, copy_share, copy_plan, grad_out, w_gate, w_up, w_down):
    rows_in, width = tokens.shape
    experts = lax.axis_size("expert")
    capacity = 2 * rows_in // experts
    owned = experts * capacity
    block_rows = 2 * owned
    placing = slot_matrix(assign, copy_share, copy_plan, experts, capacity)
    send_rows = (
        jnp.dot(placing, tokens, preferred_element_type=jnp.float32)
        .astype(jnp.bfloat16)
        .reshape(2, experts, capacity, width)
    )
    send_backs = (
        jnp.dot(placing, grad_out, preferred_element_type=jnp.float32)
        .astype(jnp.bfloat16)
        .reshape(2, experts, capacity, width)
    )
    got_rows, got_backs = (
        lax.all_to_all(send_rows, "expert", split_axis=1, concat_axis=1, tiled=True),
        lax.all_to_all(send_backs, "expert", split_axis=1, concat_axis=1, tiled=True),
    )
    all_rows, all_backs = (
        lax.all_gather(got_rows[None], "dp", axis=0, tiled=True),
        lax.all_gather(got_backs[None], "dp", axis=0, tiled=True),
    )
    ranks = all_rows.shape[0]
    all_rows = all_rows.reshape(ranks, 2, owned, width)
    all_backs = all_backs.reshape(ranks, 2, owned, width)
    copy_gate, copy_up, copy_down = copy_weights(w_gate[0], w_up[0], w_down[0], copy_plan, experts)
    gates = jnp.stack([w_gate[0], copy_gate])
    ups = jnp.stack([w_up[0], copy_up])
    downs = jnp.stack([w_down[0], copy_down])
    gate = jnp.einsum("nrcd,rdf->nrcf", all_rows, gates, preferred_element_type=jnp.float32)
    up = jnp.einsum("nrcd,rdf->nrcf", all_rows, ups, preferred_element_type=jnp.float32)
    squash = jax.nn.sigmoid(gate)
    hidden = (gate * squash * up).astype(jnp.bfloat16)
    summed_out = lax.psum_scatter(
        jnp.einsum("nrcf,rfd->nrcd", hidden, downs, preferred_element_type=jnp.float32).reshape(
            lax.axis_size("dp") * block_rows, width
        ),
        "dp",
        scatter_dimension=0,
        tiled=True,
    )
    back_out = lax.all_to_all(
        summed_out.astype(jnp.bfloat16).reshape(2, experts, capacity, width),
        "expert",
        split_axis=1,
        concat_axis=1,
        tiled=True,
    )
    grad_hidden = jnp.einsum("nrcd,rfd->nrcf", all_backs, downs, preferred_element_type=jnp.float32)
    grad_down = jnp.einsum(
        "nrcf,nrcd->rfd", hidden, all_backs, preferred_element_type=jnp.float32
    ).astype(jnp.bfloat16)
    grad_gate = (grad_hidden * up * squash * (1.0 + gate * (1.0 - squash))).astype(jnp.bfloat16)
    grad_upv = (grad_hidden * gate * squash).astype(jnp.bfloat16)
    grad_wg = jnp.einsum(
        "nrcd,nrcf->rdf", all_rows, grad_gate, preferred_element_type=jnp.float32
    ).astype(jnp.bfloat16)
    grad_wu = jnp.einsum(
        "nrcd,nrcf->rdf", all_rows, grad_upv, preferred_element_type=jnp.float32
    ).astype(jnp.bfloat16)
    result = jnp.einsum(
        "nrcf,rdf->nrcd", grad_gate, gates, preferred_element_type=jnp.float32
    ) + jnp.einsum("nrcf,rdf->nrcd", grad_upv, ups, preferred_element_type=jnp.float32)
    summed_in = lax.psum_scatter(
        result.reshape(lax.axis_size("dp") * block_rows, width),
        "dp",
        scatter_dimension=0,
        tiled=True,
    )
    back_in = lax.all_to_all(
        summed_in.astype(jnp.bfloat16).reshape(2, experts, capacity, width),
        "expert",
        split_axis=1,
        concat_axis=1,
        tiled=True,
    )
    mixed = contract_rows(placing, back_out.reshape(block_rows, width)).astype(jnp.bfloat16)
    grad_in = contract_rows(placing, back_in.reshape(block_rows, width)).astype(jnp.bfloat16)
    return (
        mixed,
        grad_in,
        grad_wg[0][None],
        grad_wu[0][None],
        grad_down[0][None],
        grad_wg[1][None],
        grad_wu[1][None],
        grad_down[1][None],
    )


def solution(mesh):
    placed = (
        P(("dp", "expert"), None),
        P(("dp", "expert"), None),
        P(("dp", "expert"), None),
        P(),
        P(("dp", "expert"), None),
        P("expert", None, "dp"),
        P("expert", None, "dp"),
        P("expert", "dp", None),
    )
    return jax.shard_map(
        body,
        mesh=mesh,
        in_specs=placed,
        out_specs=(
            P(("dp", "expert"), None),
            P(("dp", "expert"), None),
            P("expert", None, "dp"),
            P("expert", None, "dp"),
            P("expert", "dp", None),
            P("expert", None, "dp"),
            P("expert", None, "dp"),
            P("expert", "dp", None),
        ),
        check_vma=False,
    )
```

profile of v0, /device:TPU:1, one launch (start us, length us, event | category | flops | bytes accessed | tf_op | source)
XLA Modules:
  0.0 804.6 jit_solution(7412588994953115670)
XLA Ops:
  10.4 17.2 %all_to_all.30 = bf16[2,8,2,7168]{3,2,0,1:T(2,128)(2,1)S(1)} all-to-all(bf16[2,8,2,7168]{3,2,0,1:T(2,128)(2,1)S(1)} %copy.110), channel_id=1, replica_groups=mesh['dp'=16,'expert'=8] {'expert'}, dimensions={1} | all-to-all | bytes 917504 | tf_op jit(solution)/shard_map/all_to_all | solution.py:61
  27.6 0.9 copy.111
  29.0 1.1 copy.101
  30.1 3.5 all-to-all-start.2
  33.6 3.9 copy.94
  37.5 4.2 all-to-all-done.2
  42.6 2.9 pad_maximum_fusion
  45.5 35.1 %copy.95 = bf16[3,7168,128]{2,0,1:T(4,128)(2,1)} copy(bf16[3,7168,128]{2,1,0:T(8,128)(2,1)S(1)} %pad_maximum_fusion) | data formatting | bytes 11010048 | tf_op jit(solution)/shard_map/stack | solution.py:26
  80.6 5.0 all-to-all-start
  85.6 10.1 %reduce-scatter.5.cloned.1.call-start = ((), (), s32[]{:S(2)}) async-start(), calls=%async_computation.9 | async-start | bytes 15597568 | tf_op jit(solution)/shard_map/reduce_scatter | solution.py:108
  95.9 89.4 %all-to-all-done = bf16[3,7168,128]{2,0,1:T(4,128)(2,1)} async-done(((bf16[3,7168,128]{2,0,1:T(4,128)(2,1)}), bf16[3,7168,128]{2,0,1:T(4,128)(2,1)}, u32[]{:S(2)}, u32[]{:S(2)}) %all-to-all-start) | async-done | bytes 5505056 | tf_op jit(solution)/shard_map/all_to_all | solution.py:29
  185.3 6.4 copy.96
  191.7 6.3 gather_fusion
  198.0 3.1 copy.97
  201.1 3.6 bitcast_select_fusion
  204.7 34.9 %copy.98 = bf16[3,7168,128]{2,0,1:T(4,128)(2,1)S(1)} copy(bf16[3,7168,128]{2,1,0:T(8,128)(2,1)S(1)} %bitcast_select_fusion) | data formatting | bytes 11010048 | tf_op jit(solution)/shard_map/jit(_take)/select_n | solution.py:31
  239.7 89.9 %all_to_all.31 = bf16[3,7168,128]{2,0,1:T(4,128)(2,1)S(1)} all-to-all(bf16[3,7168,128]{2,0,1:T(4,128)(2,1)S(1)} %copy.98), channel_id=1, replica_groups=mesh['dp'=16,'expert'=8] {'expert'}, dimensions={1} | all-to-all | bytes 11010048 | tf_op jit(solution)/shard_map/all_to_all | solution.py:32
  329.6 10.1 %fusion.33 = (bf16[1,7168,128]{2,0,1:T(2,128)(2,1)}, bf16[1,7168,128]{2,0,1:T(2,128)(2,1)}, bf16[1,7168,128]{2,0,1:T(2,128)(2,1)}) fusion(bf16[3,7168,128]{2,0,1:T(4,128)(2,1)S(1)} %all_to_all.31), kind=kLoop, calls=%fused_computation.55 | loop fusion | bytes 11010048 | tf_op jit(solution)/shard_map/slice | solution.py:33
  339.7 8.4 %copy.124 = bf16[1,7168,128]{1,2,0:T(8,128)(2,1)} copy(bf16[1,7168,128]{2,0,1:T(2,128)(2,1)} %get-tuple-element.11) | data formatting | bytes 3670016
  348.1 3.7 copy.126
  351.8 1.5 copy.125
  353.2 14.6 %copy.112 = bf16[32,8,2,7168]{3,2,1,0:T(2,128)(2,1)} copy(bf16[32,8,2,7168]{3,1,2,0:T(8,128)(2,1)} %all-gather.7.cloned.1.call-done) | data formatting | bytes 14680064 | tf_op jit(solution)/shard_map/all_gather | solution.py:65
  367.8 15.4 %reshape.82 = bf16[16,2,16,7168]{3,2,1,0:T(8,128)(2,1)} reshape(bf16[32,8,2,7168]{3,2,1,0:T(2,128)(2,1)} %copy.112) | data formatting | bytes 14680064 | tf_op jit(solution)/shard_map/reshape | solution.py:69
  383.2 14.6 %copy.103 = bf16[32,8,2,7168]{3,2,1,0:T(2,128)(2,1)} copy(bf16[32,8,2,7168]{3,1,2,0:T(8,128)(2,1)} %all-gather.5.cloned.1.call-done) | data formatting | bytes 14680064 | tf_op jit(solution)/shard_map/all_gather | solution.py:64
  397.8 15.4 %reshape.77 = bf16[16,2,16,7168]{3,2,1,0:T(8,128)(2,1)} reshape(bf16[32,8,2,7168]{3,2,1,0:T(2,128)(2,1)} %copy.103) | data formatting | bytes 14680064 | tf_op jit(solution)/shard_map/reshape | solution.py:68
  413.3 6.4 fusion.14
  419.7 4.8 fusion.11
  424.8 2.1 multiply_convert_fusion
  427.0 7.3 fusion.10
  434.2 9.6 %add_bitcast_fusion = f32[16,2,16,7168]{3,2,0,1:T(8,128)} fusion(f32[2,7168,16,16]{1,3,2,0:T(8,128)} %fusion.10, bf16[16,2,16,128]{3,2,0,1:T(8,128)(2,1)S(1)} %get-tuple-element.20, bf16[1,7168,128]{2,1,0:T(8,128)(2,1)S(1)} %copy-done.6, bf16[1,7168,128]{2,1,0:T(8,128)(2,1)S(1)} %copy-done.5), kind=kOutput, calls=%fused_computation.1 | convolution fusion | flops 950534144 | bytes 33161216 | tf_op jit(solution)/shard_map/nrcf,rdf->nrcd/dot_general | solution.py:107
  443.8 12.0 %copy.114 = f32[16,2,16,7168]{3,2,1,0:T(8,128)} copy(f32[16,2,16,7168]{3,2,0,1:T(8,128)} %add_bitcast_fusion) | data formatting | bytes 29360128 | tf_op jit(solution)/shard_map/add | solution.py:105
  456.2 1.2 copy-done.8
  457.3 9.1 %convolution_bitcast_fusion = f32[16,2,16,7168]{3,2,0,1:T(8,128)} fusion(bf16[16,2,16,128]{3,2,0,1:T(8,128)(2,1)S(1)} %get-tuple-element.22, bf16[1,128,7168]{2,1,0:T(8,128)(2,1)} %bitcast.87, bf16[1,128,7168]{2,1,0:T(8,128)(2,1)S(1)} %copy-done.8), kind=kOutput, calls=%fused_computation.2 | convolution fusion | flops 946864128 | bytes 18481152 | tf_op jit(solution)/shard_map/nrcf,rfd->nrcd/dot_general | solution.py:79
  466.4 12.2 %copy.107 = f32[16,2,16,7168]{3,2,1,0:T(8,128)} copy(f32[16,2,16,7168]{3,2,0,1:T(8,128)} %convolution_bitcast_fusion) | data formatting | bytes 29360128 | tf_op jit(solution)/shard_map/nrcf,rfd->nrcd/transpose | solution.py:79
  478.7 6.2 fusion.2
  484.9 3.0 fusion.1
  487.9 3.2 fusion.35
  491.0 124.5 %reduce-scatter.5.cloned.1.call-done = f32[32,7168]{1,0:T(8,128)} async-done(((f32[512,7168]{1,0:T(8,128)}), f32[32,7168]{1,0:T(8,128)}) %reduce-scatter.5.cloned.1.call-update) | async-done | bytes 917520 | tf_op jit(solution)/shard_map/reduce_scatter | solution.py:108
  615.6 1.2 convert_element_type.49
  617.0 1.1 copy.115
  618.1 6.6 all-to-all-start.5
  624.7 6.7 fusion
  631.4 148.0 %reduce-scatter.3.cloned.1.call-done = f32[32,7168]{1,0:T(8,128)} async-done(((f32[512,7168]{1,0:T(8,128)}), f32[32,7168]{1,0:T(8,128)}) %reduce-scatter.3.cloned.1.call-update) | async-done | bytes 917520 | tf_op jit(solution)/shard_map/reduce_scatter | solution.py:78
  779.4 1.2 convert_element_type.44
  780.8 1.1 copy.108
  781.9 6.1 all-to-all-start.3
  788.0 4.2 fusion.34
  793.5 2.6 all-to-all-done.3
  (74 shorter events, 8.5 us)
Async XLA Ops:
  7.2 2.4 copy-start
  7.2 21.4 %copy-start.12 = (bf16[8,7168]{1,0:T(8,128)(2,1)S(1)}, bf16[8,7168]{1,0:T(8,128)(2,1)}, u32[]{:S(2)}) copy-start(bf16[8,7168]{1,0:T(8,128)(2,1)} %param.8) | copy-start | bytes 344068
  7.2 346.0 %all-gather.7.cloned.1.call-start = ((), (), s32[]{:S(2)}) async-start(), calls=%async_computation.11 | async-start | bytes 7798784 | tf_op jit(solution)/shard_map/all_gather | solution.py:65
  9.6 19.2 %copy-start.13 = (s32[8]{0:T(128)}, s32[8]{0:T(128)S(1)}, u32[]{:S(2)}) copy-start(s32[8]{0:T(128)S(1)} %compare_select_fusion.1) | copy-start | bytes 100
  29.0 13.6 %copy-start.3 = (bf16[1,7168,128]{2,1,0:T(8,128)(2,1)S(1)}, bf16[1,7168,128]{2,1,0:T(8,128)(2,1)}, u32[]{:S(2)}) copy-start(bf16[1,7168,128]{2,1,0:T(8,128)(2,1)} %param.13) | copy-start | bytes 5505028
  30.1 11.6 %all-to-all-start.2 = ((bf16[2,8,2,7168]{3,2,0,1:T(2,128)(2,1)}), bf16[2,8,2,7168]{3,2,0,1:T(2,128)(2,1)S(1)}, u32[]{:S(2)}, u32[]{:S(2)}) async-start(bf16[2,8,2,7168]{3,2,0,1:T(2,128)(2,1)} %copy.101), calls=%async_computation.2 | async-start | bytes 917504 | tf_op jit(solution)/shard_map/all_to_all | solution.py:60
  33.6 349.6 %all-gather.5.cloned.1.call-start = ((), (), s32[]{:S(2)}) async-start(), calls=%async_computation.10 | async-start | bytes 7798784 | tf_op jit(solution)/shard_map/all_gather | solution.py:64
  80.6 15.2 %copy-start.15 = (s32[8]{0:T(128)S(1)}, s32[8]{0:T(128)}, u32[]{:S(2)}) copy-start(s32[8]{0:T(128)} %param.11) | copy-start | bytes 100
  80.6 104.7 %all-to-all-start = ((bf16[3,7168,128]{2,0,1:T(4,128)(2,1)}), bf16[3,7168,128]{2,0,1:T(4,128)(2,1)}, u32[]{:S(2)}, u32[]{:S(2)}) async-start(bf16[3,7168,128]{2,0,1:T(4,128)(2,1)} %copy.95), calls=%async_computation | async-start | bytes 14680064 | tf_op jit(solution)/shard_map/all_to_all | solution.py:29
  85.6 529.9 %reduce-scatter.5.cloned.1.call-start = ((), (), s32[]{:S(2)}) async-start(), calls=%async_computation.9 | async-start | bytes 15597568 | tf_op jit(solution)/shard_map/reduce_scatter | solution.py:108
  348.1 3.7 copy-start.2
  413.3 6.4 copy-start.4
  413.3 11.3 %slice-start = ((s8[7340032]{0:T(1024)(128)(4,1)}), s8[4194304]{0:T(1024)(128)(4,1)S(1)}, s32[]{:S(2)}) async-start(s8[7340032]{0:T(1024)(128)(4,1)} %bitcast.80), calls=%async_computation.12 | async-start | bytes 8388608
  419.7 4.9 slice-start.1
  419.7 4.9 copy-start.7
  419.7 5.1 copy-start.9
  426.9 7.3 copy-start.10
  427.0 7.3 copy-start.5
  427.0 7.3 copy-start.6
  455.8 1.5 copy-start.8
  455.9 323.5 %reduce-scatter.3.cloned.1.call-start = ((), (), s32[]{:S(2)}) async-start(), calls=%async_computation.8 | async-start | bytes 15597568 | tf_op jit(solution)/shard_map/reduce_scatter | solution.py:78
  478.6 6.3 slice-start.2
  478.6 6.2 slice-start.3
  478.7 6.2 copy-start.11
  618.1 163.8 %all-to-all-start.5 = ((bf16[2,8,2,7168]{3,2,0,1:T(2,128)(2,1)}), bf16[2,8,2,7168]{3,2,0,1:T(2,128)(2,1)S(1)}, u32[]{:S(2)}, u32[]{:S(2)}) async-start(bf16[2,8,2,7168]{3,2,0,1:T(2,128)(2,1)} %copy.115), calls=%async_computation.7 | async-start | bytes 917504 | tf_op jit(solution)/shard_map/all_to_all | solution.py:114
  781.9 14.3 %all-to-all-start.3 = ((bf16[2,8,2,7168]{3,2,0,1:T(2,128)(2,1)}), bf16[2,8,2,7168]{3,2,0,1:T(2,128)(2,1)S(1)}, u32[]{:S(2)}, u32[]{:S(2)}) async-start(bf16[2,8,2,7168]{3,2,0,1:T(2,128)(2,1)} %copy.108), calls=%async_computation.4 | async-start | bytes 917504 | tf_op jit(solution)/shard_map/all_to_all | solution.py:86
  787.9 4.7 copy-start.14
  788.0 9.6 %copy-start.1 = (bf16[8,7168]{1,0:T(8,128)(2,1)S(1)}, bf16[8,7168]{1,0:T(8,128)(2,1)}, u32[]{:S(2)}) copy-start(bf16[8,7168]{1,0:T(8,128)(2,1)} %param.12) | copy-start | bytes 344068
Sparse Core Ops, SparseCore 0:
  28.7 49.5 all-gather.6
  80.5 122.1 all-gather.4
  456.0 159.5 reduce-scatter.4
  617.8 161.4 reduce-scatter.2
where the time goes:
time: 813 us; the launch traced here: 805 us
  waiting for transfers between devices  369 us (45%)
  local copies, waits for them, and re-layouts  214 us (26%)
  blocking collectives  107 us (13%)
  matrix products  57.4 us (7%)
  starting transfers between devices  31.7 us (4%)
  between operations  14.7 us (2%)
  other arithmetic  11.4 us (1%)
    reduce_scatter x1, waiting for transfers between devices, body(): lax.psum_scatter(jnp.einsum('nrcf,rfd->nrcd', hidden, downs, preferred_el...  148 us
    reduce_scatter x1, waiting for transfers between devices, body(): lax.psum_scatter(result.reshape(lax.axis_size('dp') * block_rows, width),...  125 us
    all_to_all x1, blocking collectives, copy_weights(): lax.all_to_all(chosen, 'expert', split_axis=1, concat_axis=1, tiled=True)  89.9 us
    all_to_all x1, waiting for transfers between devices, copy_weights(): lax.all_to_all(stacked, 'expert', split_axis=1, concat_axis=1, tiled=True)  89.4 us
    another operation x1, local copies, waits for them, and re-layouts, copy_weights(): stacked = jnp.stack([gate_w, up_w, down_w.T])  35.1 us
    select_n x1, local copies, waits for them, and re-layouts, copy_weights(): chosen = jnp.take(pieces, copy_plan, axis=1).reshape(3, width, units)  34.9 us
    unnamed x44, local copies, waits for them, and re-layouts  18.9 us
    all_to_all x1, blocking collectives, body(): lax.all_to_all(send_backs, 'expert', split_axis=1, concat_axis=1, tiled=T...  17.2 us
  transfers between devices with their start and end apart: 8, of which 5 were waited for; matrix products, arithmetic and copies ran while one was open for 25% of the time, Pallas kernels for 0%

commit v1 on v0

v1 whole, which is shorter than its diff:
```python
import functools

import jax
import jax.numpy as jnp
from jax import lax
from jax.experimental import pallas as pl
from jax.experimental.pallas import tpu as pltpu
from jax.sharding import PartitionSpec as P

MESH = pl.DeviceIdType.MESH
BF16 = jnp.bfloat16
F32 = jnp.float32
LANES = 128


def dot(a, b):
    return jnp.dot(a, b, preferred_element_type=F32)


def dot_nt(a, b):
    return lax.dot_general(a, b, (((1,), (1,)), ((), ())), preferred_element_type=F32)


def dot_tn(a, b):
    return lax.dot_general(a, b, (((0,), (0,)), ((), ())), preferred_element_type=F32)


def kernel(
    experts,
    half,
    part_p,
    chunk,
    plan_ref,
    ext_ref,
    w_gate,
    w_up,
    w_down,
    o_out,
    gate_out,
    up_out,
    down_out,
    copy_gate_out,
    copy_up_out,
    copy_down_out,
    raw,
    a2a_send,
    a2a_recv,
    own,
    cpy,
    w1,
    wd,
    pre,
    pre_recv,
    acts,
    gx1,
    gx2s,
    gx2,
    gcat,
    hcat,
    part,
    rz,
    rxo,
    rxf,
    ro_q,
    rf_q,
    rzq,
    fin,
    back_send,
    back_recv,
    outs,
    st1,
    st2,
    ct1,
    ct2,
    ssem,
    rsem,
    lsem,
):
    units = w1.shape[2] // 2
    full = half + LANES
    per_chip = 4 * experts
    slots = 8 * per_chip
    block = 2 * per_chip
    mid = block // 2
    steps = half // chunk
    part_q = half - part_p

    dp = lax.axis_index("dp")
    ex = lax.axis_index("expert")
    x = dp // 4
    z = (dp // 2) % 2
    c = dp % 2
    o = 1 - c

    def chip(dx, zz):
        return lax.rem(x + dx, 4) * 2 + zz

    me = chip(0, z)
    xp = (lax.rem(dp + 4, 16), ex)
    xm = (lax.rem(dp + 12, 16), ex)
    zp = (dp + 2 - 4 * z, ex)
    sib = (dp + 1 - 2 * c, ex)

    def peer(i):
        return (dp, lax.rem(ex + i, experts))

    used = [0]
    sends = []

    def fresh():
        used[0] += 1
        return used[0] - 1

    def msg(k, src, dst, dev):
        copy = pltpu.make_async_remote_copy(
            src_ref=src,
            dst_ref=dst,
            send_sem=ssem.at[k],
            recv_sem=rsem.at[k],
            device_id=dev,
            device_id_type=MESH,
        )
        copy.start()
        sends.append(copy)

    def got(k, ref, dev):
        pltpu.make_async_remote_copy(
            src_ref=ref,
            dst_ref=ref,
            send_sem=ssem.at[k],
            recv_sem=rsem.at[k],
            device_id=dev,
            device_id_type=MESH,
        ).wait_recv()

    used_local = [0]

    def local(src, dst):
        copy = pltpu.make_async_copy(src, dst, lsem.at[used_local[0]])
        used_local[0] += 1
        copy.start()
        return copy

    my_rows = pl.ds(pl.multiple_of(c * half, half), half)
    other_rows = pl.ds(pl.multiple_of(o * half, half), half)

    weight_loads = [
        local(w_gate.at[0, my_rows, :], w1.at[0, :, pl.ds(0, units)]),
        local(w_up.at[0, my_rows, :], w1.at[0, :, pl.ds(units, units)]),
        local(w_down.at[0, :, my_rows], wd.at[pl.ds(0, units), :]),
    ]

    barrier = pltpu.get_barrier_semaphore()
    greeted = [xp, xm, zp, sib] + [peer(i) for i in range(1, experts)]
    for dev in greeted:
        pl.semaphore_signal(barrier, inc=1, device_id=dev, device_id_type=MESH)
    pl.semaphore_wait(barrier, len(greeted))

    k_raw = fresh()
    msg(k_raw, ext_ref.at[o], raw.at[c], sib)
    k_w = [fresh() for _ in range(3)]
    msg(k_w[0], w_gate.at[0, other_rows, :], w1.at[1, :, pl.ds(0, units)], sib)
    msg(k_w[1], w_up.at[0, other_rows, :], w1.at[1, :, pl.ds(units, units)], sib)
    msg(k_w[2], w_down.at[0, :, other_rows], wd.at[pl.ds(units, units), :], sib)
    raw[c] = ext_ref[c]
    got(k_raw, raw.at[o], sib)

    placed = raw[:, :, half:full].reshape(32, LANES)[:, : 16 * experts]
    rows = raw[...].reshape(32, full)
    a2a_send[...] = dot_tn(placed, rows).astype(BF16).reshape(experts, 16, full)
    k_a2a = [fresh() for _ in range(experts - 1)]
    for i in range(1, experts):
        dev = peer(i)
        msg(k_a2a[i - 1], a2a_send.at[dev[1]], a2a_recv.at[ex], dev)
    a2a_recv[ex] = a2a_send[ex]
    for i in range(1, experts):
        got(k_a2a[i - 1], a2a_recv.at[lax.rem(ex + experts - i, experts)], peer(i))

    size = 16 * experts
    to = lax.broadcasted_iota(jnp.int32, (size, size), 0)
    fr = lax.broadcasted_iota(jnp.int32, (size, size), 1)
    want = (
        ((fr // 8) % 2) * block + ((fr // 4) % 2) * per_chip + (fr // 16) * 4 + fr % 4
    )
    moved = dot((to == want).astype(BF16), a2a_recv[...].reshape(size, full)).astype(BF16)
    own[me] = moved[:block]
    cpy[me] = moved[block:, :half]

    def gather(buf, width):
        keys = [fresh() for _ in range(18)]

        def cut(q, lane, row=None):
            start, count = (0, block) if row is None else (row * mid, mid)
            if lane == 0:
                return buf.at[q, pl.ds(start, count), pl.ds(0, part_p)]
            return buf.at[q, pl.ds(start, count), pl.ds(part_p, width - part_p)]

        y = 1 - z

        def first():
            msg(keys[9], cut(me, 1), cut(me, 1), zp)
            msg(keys[0], cut(me, 0), cut(me, 0), xp)
            msg(keys[1], cut(me, 0), cut(me, 0), xm)
            msg(keys[2], cut(me, 0), cut(me, 0), zp)
            msg(keys[10], cut(me, 1), cut(me, 1), xp)
            msg(keys[11], cut(me, 1), cut(me, 1), xm)

        def second():
            got(keys[9], cut(chip(0, y), 1), zp)
            msg(keys[12], cut(chip(0, y), 1), cut(chip(0, y), 1), xp)
            msg(keys[13], cut(chip(0, y), 1), cut(chip(0, y), 1), xm)
            got(keys[0], cut(chip(3, z), 0), xm)
            msg(keys[3], cut(chip(3, z), 0, 0), cut(chip(3, z), 0, 0), xp)
            msg(keys[5], cut(chip(3, z), 0), cut(chip(3, z), 0), zp)
            got(keys[1], cut(chip(1, z), 0), xp)
            msg(keys[4], cut(chip(1, z), 0, 1), cut(chip(1, z), 0, 1), xm)
            msg(keys[6], cut(chip(1, z), 0), cut(chip(1, z), 0), zp)

        def third():
            got(keys[10], cut(chip(3, z), 1), xm)
            msg(keys[14], cut(chip(3, z), 1, 0), cut(chip(3, z), 1, 0), xp)
            got(keys[11], cut(chip(1, z), 1), xp)
            msg(keys[15], cut(chip(1, z), 1, 1), cut(chip(1, z), 1, 1), xm)
            got(keys[3], cut(chip(2, z), 0, 0), xm)
            msg(keys[7], cut(chip(2, z), 0, 0), cut(chip(2, z), 0, 0), zp)
            got(keys[4], cut(chip(2, z), 0, 1), xp)
            msg(keys[8], cut(chip(2, z), 0, 1), cut(chip(2, z), 0, 1), zp)
            got(keys[12], cut(chip(3, y), 1), xm)
            msg(keys[16], cut(chip(3, y), 1, 0), cut(chip(3, y), 1, 0), xp)
            got(keys[13], cut(chip(1, y), 1), xp)
            msg(keys[17], cut(chip(1, y), 1, 1), cut(chip(1, y), 1, 1), xm)

        def last():
            got(keys[2], cut(chip(0, y), 0), zp)
            got(keys[5], cut(chip(3, y), 0), zp)
            got(keys[6], cut(chip(1, y), 0), zp)
            got(keys[14], cut(chip(2, z), 1, 0), xm)
            got(keys[15], cut(chip(2, z), 1, 1), xp)
            got(keys[7], cut(chip(2, y), 0, 0), zp)
            got(keys[8], cut(chip(2, y), 0, 1), zp)
            got(keys[16], cut(chip(2, y), 1, 0), xm)
            got(keys[17], cut(chip(2, y), 1, 1), xp)

        return first, second, third, last

    own_first, own_second, own_third, own_last = gather(own, full)
    cpy_first, cpy_second, cpy_third, cpy_last = gather(cpy, half)
    own_first()
    own_second()
    own_third()
    cpy_first()

    for load in weight_loads:
        load.wait()
    got(k_w[0], w1.at[1, :, pl.ds(0, units)], sib)
    got(k_w[1], w1.at[1, :, pl.ds(units, units)], sib)
    got(k_w[2], wd.at[pl.ds(units, units), :], sib)
    own_last()

    pre[...] = jnp.zeros_like(pre)

    def tokens_of(buf, cols):
        return buf[:, :per_chip, cols].reshape(slots, chunk)

    def backs_of(buf, cols):
        return buf[:, per_chip:, cols].reshape(slots, chunk)

    @pl.loop(0, steps)
    def _(step):
        cols = pl.ds(pl.multiple_of(step * chunk, chunk), chunk)
        t = tokens_of(own, cols)
        g = backs_of(own, cols)
        pre[0, :, : 2 * units] += dot(t, w1[0, cols, :])
        pre[1, :, : 2 * units] += dot(t, w1[1, cols, :])
        gh = dot_nt(g, wd[:, cols])
        pre[0, :, 2 * units :] += gh[:, :units]
        pre[1, :, 2 * units :] += gh[:, units:]

    k_pre = fresh()
    msg(k_pre, pre.at[1], pre_recv, sib)
    cpy_second()
    got(k_pre, pre_recv, sib)
    total = pre[0] + pre_recv[...]
    gate = total[:, :units]
    up = total[:, units : 2 * units]
    grad_hidden = total[:, 2 * units :]
    squash = jax.nn.sigmoid(gate)
    acts[0, :, :units] = (gate * squash * up).astype(BF16)
    acts[0, :, units : 2 * units] = (
        grad_hidden * up * squash * (1.0 + gate * (1.0 - squash))
    ).astype(BF16)
    acts[0, :, 2 * units :] = (grad_hidden * gate * squash).astype(BF16)
    k_acts = fresh()
    msg(k_acts, acts.at[0], acts.at[1], sib)

    k_gx1 = [fresh() for _ in range(experts - 1)]
    for i in range(1, experts):
        dev = peer(i)
        piece = pl.ds(pl.multiple_of(dev[1] * (slots // experts), slots // experts), slots // experts)
        msg(k_gx1[i - 1], acts.at[0, piece, :], gx1.at[ex], dev)
    piece = pl.ds(pl.multiple_of(ex * (slots // experts), slots // experts), slots // experts)
    gx1[ex] = acts[0, piece, :]

    got(k_acts, acts.at[1], sib)
    hcat[:, :units] = acts[0, :, :units]
    hcat[:, units:] = acts[1, :, :units]

    @pl.loop(0, steps)
    def _(step):
        cols = pl.ds(pl.multiple_of(step * chunk, chunk), chunk)
        m = dot(hcat[...], wd[:, cols])
        part[:, :per_chip, cols] = m.astype(BF16).reshape(8, per_chip, chunk)
        r = dot_nt(acts[0, :, units:], w1[0, cols, :]) + dot_nt(acts[1, :, units:], w1[1, cols, :])
        part[:, per_chip:, cols] = r.astype(BF16).reshape(8, per_chip, chunk)

    cols_p = pl.ds(0, part_p)
    cols_q = pl.ds(part_p, part_q)
    first_rows = pl.ds(0, mid)
    last_rows = pl.ds(mid, mid)
    every = pl.ds(0, block)
    y = 1 - z

    k_z = [fresh() for _ in range(4)]
    k_xo = [fresh() for _ in range(2)]
    k_xf = [fresh() for _ in range(2)]
    k_yo = [[fresh() for _ in range(2)] for _ in range(2)]
    k_yf = [[fresh() for _ in range(2)] for _ in range(2)]
    k_w0 = fresh()

    def add(ref, extra):
        ref[...] = (ref[...].astype(F32) + extra[...].astype(F32)).astype(BF16)

    for j in (2, 1, 3, 0):
        msg(k_z[j], part.at[chip(j, y), every, cols_p], rz.at[j], zp)
    for i, zz in enumerate((y, z)):
        msg(k_yo[i][0], part.at[chip(2, zz), first_rows, cols_q], ro_q.at[i, 0], xp)
        msg(k_yo[i][1], part.at[chip(2, zz), last_rows, cols_q], ro_q.at[i, 1], xm)
    cpy_third()

    for i in range(1, experts):
        got(k_gx1[i - 1], gx1.at[lax.rem(ex + experts - i, experts)], peer(i))
    for i in range(experts):
        gx2s[i] = gx1[plan_ref[i]]
    k_gx2 = [fresh() for _ in range(experts - 1)]
    for i in range(1, experts):
        dev = peer(i)
        msg(k_gx2[i - 1], gx2s.at[dev[1]], gx2.at[0, ex], dev)
    gx2[0, ex] = gx2s[ex]

    marks = own[:, :per_chip, half:full].reshape(slots, LANES).astype(F32)
    lane = lax.broadcasted_iota(jnp.int32, (slots, LANES), 1)
    copied = jnp.sum(jnp.where((lane // 8) % 2 == 1, marks, 0.0), axis=1, keepdims=True)
    kept = 1.0 - copied
    gcat[:, : 2 * units] = (acts[0, :, units:].astype(F32) * kept).astype(BF16)
    gcat[:, 2 * units :] = (acts[1, :, units:].astype(F32) * kept).astype(BF16)
    hcat[...] = (hcat[...].astype(F32) * kept).astype(BF16)

    def weight_grads(buf, one, two):
        @pl.loop(0, steps)
        def _(step):
            cols = pl.ds(pl.multiple_of(step * chunk, chunk), chunk)
            d = dot_tn(tokens_of(buf, cols), gcat[...]).astype(BF16)
            one[0, cols, :] = d[:, : 2 * units]
            one[1, cols, :] = d[:, 2 * units :]
            two[:, cols] = dot_tn(hcat[...], backs_of(buf, cols)).astype(BF16)

    def write_grads(one, two, g_out, u_out, d_out):
        keys = [fresh() for _ in range(3)]
        lanes_g, lanes_u = pl.ds(0, units), pl.ds(units, units)
        msg(keys[0], one.at[1, :, lanes_g], g_out.at[0, my_rows, :], sib)
        msg(keys[1], one.at[1, :, lanes_u], u_out.at[0, my_rows, :], sib)
        msg(keys[2], two.at[lanes_u, :], d_out.at[0, :, my_rows], sib)
        mine = [
            local(one.at[0, :, lanes_g], g_out.at[0, my_rows, :]),
            local(one.at[0, :, lanes_u], u_out.at[0, my_rows, :]),
            local(two.at[lanes_g, :], d_out.at[0, :, my_rows]),
        ]

        def finish():
            for copy in mine:
                copy.wait()
            got(keys[0], g_out.at[0, other_rows, :], sib)
            got(keys[1], u_out.at[0, other_rows, :], sib)
            got(keys[2], d_out.at[0, :, other_rows], sib)

        return finish

    weight_grads(own, st1, st2)
    finish_own = write_grads(st1, st2, gate_out, up_out, down_out)

    for i, zz in enumerate((y, z)):
        got(k_yo[i][0], ro_q.at[i, 0], xm)
        add(part.at[chip(1, zz), first_rows, cols_q], ro_q.at[i, 0])
        msg(k_yf[i][0], part.at[chip(1, zz), every, cols_q], rf_q.at[i, 0], xp)
        got(k_yo[i][1], ro_q.at[i, 1], xp)
        add(part.at[chip(3, zz), last_rows, cols_q], ro_q.at[i, 1])
        msg(k_yf[i][1], part.at[chip(3, zz), every, cols_q], rf_q.at[i, 1], xm)
    got(k_z[2], rz.at[2], zp)
    add(part.at[chip(2, z), every, cols_p], rz.at[2])
    msg(k_xo[0], part.at[chip(2, z), first_rows, cols_p], rxo.at[0], xp)
    msg(k_xo[1], part.at[chip(2, z), last_rows, cols_p], rxo.at[1], xm)
    got(k_z[1], rz.at[1], zp)
    add(part.at[chip(1, z), every, cols_p], rz.at[1])
    got(k_z[3], rz.at[3], zp)
    add(part.at[chip(3, z), every, cols_p], rz.at[3])
    got(k_xo[0], rxo.at[0], xm)
    add(part.at[chip(1, z), first_rows, cols_p], rxo.at[0])
    msg(k_xf[0], part.at[chip(1, z), every, cols_p], rxf.at[0], xp)
    got(k_xo[1], rxo.at[1], xp)
    add(part.at[chip(3, z), last_rows, cols_p], rxo.at[1])
    msg(k_xf[1], part.at[chip(3, z), every, cols_p], rxf.at[1], xm)

    got(k_yf[0][0], rf_q.at[0, 0], xm)
    got(k_yf[0][1], rf_q.at[0, 1], xp)
    mine_y = part.at[chip(0, y), every, cols_q]
    mine_y[...] = (
        mine_y[...].astype(F32) + rf_q[0, 0].astype(F32) + rf_q[0, 1].astype(F32)
    ).astype(BF16)
    msg(k_w0, mine_y, rzq, zp)

    cpy_last()
    for i in range(1, experts):
        got(k_gx2[i - 1], gx2.at[0, lax.rem(ex + experts - i, experts)], peer(i))
    k_gsib = fresh()
    msg(k_gsib, gx2.at[0], gx2.at[1], sib)

    got(k_z[0], rz.at[0], zp)
    got(k_xf[0], rxf.at[0], xm)
    got(k_xf[1], rxf.at[1], xp)
    fin[:, cols_p] = (
        part[me, :, cols_p].astype(F32)
        + rz[0].astype(F32)
        + rxf[0].astype(F32)
        + rxf[1].astype(F32)
    ).astype(BF16)
    got(k_yf[1][0], rf_q.at[1, 0], xm)
    got(k_yf[1][1], rf_q.at[1, 1], xp)
    got(k_w0, rzq, zp)
    fin[:, cols_q] = (
        part[me, :, cols_q].astype(F32)
        + rf_q[1, 0].astype(F32)
        + rf_q[1, 1].astype(F32)
        + rzq[...].astype(F32)
    ).astype(BF16)

    to = lax.broadcasted_iota(jnp.int32, (size, block), 0)
    fr = lax.broadcasted_iota(jnp.int32, (size, block), 1)
    want = (to // 16) * 4 + ((to // 4) % 2) * per_chip + to % 4
    side = (to // 8) % 2
    quarter = half // 2
    back_send[...] = (
        dot(jnp.logical_and(fr == want, side == 0).astype(BF16), fin[:, :quarter])
        + dot(jnp.logical_and(fr == want, side == 1).astype(BF16), fin[:, quarter:])
    ).astype(BF16).reshape(experts, 16, quarter)
    k_back = [fresh() for _ in range(experts - 1)]
    for i in range(1, experts):
        dev = peer(i)
        msg(k_back[i - 1], back_send.at[dev[1]], back_recv.at[ex], dev)
    back_recv[ex] = back_send[ex]

    got(k_gsib, gx2.at[1], sib)
    for i in range(2):
        gcat[:, 2 * units * i : 2 * units * (i + 1)] = gx2[i, :, :, units:].reshape(
            slots, 2 * units
        )
        hcat[:, units * i : units * (i + 1)] = gx2[i, :, :, :units].reshape(slots, units)
    weight_grads(cpy, ct1, ct2)
    finish_cpy = write_grads(ct1, ct2, copy_gate_out, copy_up_out, copy_down_out)

    for i in range(1, experts):
        got(k_back[i - 1], back_recv.at[lax.rem(ex + experts - i, experts)], peer(i))
    spots = raw[:, :, half:full].reshape(32, LANES).astype(F32)
    lane = lax.broadcasted_iota(jnp.int32, (32, LANES), 1)
    spots = jnp.where((lane // 8) % 2 == 0, spots, 0.0)
    later = pltpu.roll(spots, 8, 1)
    got_back = back_recv[...].reshape(size, quarter)
    outs[:, :, :quarter] = (
        dot(spots[:, :size].astype(BF16), got_back).astype(BF16).reshape(2, 16, quarter)
    )
    outs[:, :, quarter:] = (
        dot(later[:, :size].astype(BF16), got_back).astype(BF16).reshape(2, 16, quarter)
    )
    k_out = fresh()
    msg(k_out, outs.at[o], o_out.at[c], sib)
    mine_out = local(outs.at[c], o_out.at[c])
    mine_out.wait()
    got(k_out, o_out.at[o], sib)
    finish_own()
    finish_cpy()
    for copy in sends:
        copy.wait_send()


def placing(assign, copy_share, copy_plan, experts):
    expert_of = assign[:, 0]
    numbers = jnp.arange(experts, dtype=jnp.int32)
    onehot = (expert_of[:, None] == numbers[None, :]).astype(jnp.int32)
    before = jnp.cumsum(onehot, axis=0) - onehot
    rank_in = jnp.sum(before * onehot, axis=1)
    limit_rows = jnp.sum(copy_share[0][None, :] * onehot, axis=1)
    holder = jnp.sum(
        numbers[None, :] * (copy_plan[None, :] == expert_of[:, None]).astype(jnp.int32), axis=1
    )
    core = lax.rem(lax.axis_index("dp"), 2)
    array = jnp.arange(2, dtype=jnp.int32)[:, None]
    spot = array * 4 + core * 2 + rank_in[None, :]
    owned = expert_of[None, :] * 16 + spot
    copied = jnp.where((rank_in < limit_rows)[None, :], holder[None, :] * 16 + 8 + spot, -1)
    places = jnp.arange(LANES, dtype=jnp.int32)
    hit = jnp.logical_or(places == owned[:, :, None], places == copied[:, :, None])
    return hit.astype(BF16).reshape(-1, LANES)


def body(tokens, assign, copy_share, copy_plan, grad_out, w_gate, w_up, w_down):
    rows_in, width = tokens.shape
    experts = lax.axis_size("expert")
    units = w_gate.shape[2]
    half = width // 2
    full = half + LANES
    chunk = half // 7
    part_p = 3 * chunk
    per_chip = 4 * experts
    slots = 8 * per_chip
    block = 2 * per_chip
    mid = block // 2
    marks = placing(assign, copy_share, copy_plan, experts)
    both = jnp.concatenate([tokens, grad_out], axis=0)
    ext = jnp.stack(
        [
            jnp.concatenate([both[:, :half], marks], axis=1),
            jnp.concatenate([both[:, half:], marks], axis=1),
        ]
    )
    vmem = pltpu.VMEM
    part_q = half - part_p
    messages = 128
    any_spec = pl.BlockSpec(memory_space=pl.ANY)
    o, g, u, d, cg, cu, cd = pl.pallas_call(
        functools.partial(kernel, experts, half, part_p, chunk),
        out_shape=[
            jax.ShapeDtypeStruct((2, 16, half), BF16),
            jax.ShapeDtypeStruct(w_gate.shape, BF16),
            jax.ShapeDtypeStruct(w_up.shape, BF16),
            jax.ShapeDtypeStruct(w_down.shape, BF16),
            jax.ShapeDtypeStruct(w_gate.shape, BF16),
            jax.ShapeDtypeStruct(w_up.shape, BF16),
            jax.ShapeDtypeStruct(w_down.shape, BF16),
        ],
        in_specs=[
            pl.BlockSpec(memory_space=pltpu.SMEM),
            pl.BlockSpec(memory_space=pltpu.VMEM),
            any_spec,
            any_spec,
            any_spec,
        ],
        out_specs=[any_spec] * 7,
        scratch_shapes=[
            vmem((2, 16, full), BF16),
            vmem((experts, 16, full), BF16),
            vmem((experts, 16, full), BF16),
            vmem((8, block, full), BF16),
            vmem((8, block, half), BF16),
            vmem((2, half, 2 * units), BF16),
            vmem((2 * units, half), BF16),
            vmem((2, slots, 3 * units), F32),
            vmem((slots, 3 * units), F32),
            vmem((2, slots, 3 * units), BF16),
            vmem((experts, slots // experts, 3 * units), BF16),
            vmem((experts, slots // experts, 3 * units), BF16),
            vmem((2, experts, slots // experts, 3 * units), BF16),
            vmem((slots, 4 * units), BF16),
            vmem((slots, 2 * units), BF16),
            vmem((8, block, half), BF16),
            vmem((4, block, part_p), BF16),
            vmem((2, mid, part_p), BF16),
            vmem((2, block, part_p), BF16),
            vmem((2, 2, mid, part_q), BF16),
            vmem((2, 2, block, part_q), BF16),
            vmem((block, part_q), BF16),
            vmem((block, half), BF16),
            vmem((experts, 16, half // 2), BF16),
            vmem((experts, 16, half // 2), BF16),
            vmem((2, 16, half), BF16),
            vmem((2, half, 2 * units), BF16),
            vmem((2 * units, half), BF16),
            vmem((2, half, 2 * units), BF16),
            vmem((2 * units, half), BF16),
            pltpu.SemaphoreType.DMA((messages,)),
            pltpu.SemaphoreType.DMA((messages,)),
            pltpu.SemaphoreType.DMA((16,)),
        ],
        compiler_params=pltpu.CompilerParams(
            collective_id=0,
            has_side_effects=True,
            vmem_limit_bytes=56 * 1024 * 1024,
        ),
        cost_estimate=pl.CostEstimate(
            flops=6_000_000_000, bytes_accessed=30_000_000, transcendentals=32768
        ),
    )(copy_plan, ext, w_gate, w_up, w_down)
    mixed = jnp.concatenate([o[0, :rows_in], o[1, :rows_in]], axis=1)
    grad_in = jnp.concatenate([o[0, rows_in:], o[1, rows_in:]], axis=1)
    return (mixed, grad_in, g, u, d, cg, cu, cd)


def solution(mesh):
    placed = (
        P(("dp", "expert"), None),
        P(("dp", "expert"), None),
        P(("dp", "expert"), None),
        P(),
        P(("dp", "expert"), None),
        P("expert", None, "dp"),
        P("expert", None, "dp"),
        P("expert", "dp", None),
    )
    return jax.shard_map(
        body,
        mesh=mesh,
        in_specs=placed,
        out_specs=(
            P(("dp", "expert"), None),
            P(("dp", "expert"), None),
            P("expert", None, "dp"),
            P("expert", None, "dp"),
            P("expert", "dp", None),
            P("expert", None, "dp"),
            P("expert", None, "dp"),
            P("expert", "dp", None),
        ),
        check_vma=False,
    )
```

time: 813 us -> 138 us (0.17); the launches traced: 805 us -> 138 us
  waiting for transfers between devices: 369 us -> 0 us
  local copies, waits for them, and re-layouts: 214 us -> 16.1 us
  Pallas kernels: 0 us -> 117 us
  blocking collectives: 107 us -> 0 us
  matrix products: 57.4 us -> 0 us
  starting transfers between devices: 31.7 us -> 0 us
  between operations: 14.7 us -> 0.7 us
    reduce_scatter x2 -> x0, waiting for transfers between devices: 272 us -> none  [the longest x1 148 us: body(): lax.psum_scatter(jnp.einsum('nrcf,rfd->nrcd', hidden, downs, preferred_el...]
    pallas_call x0 -> x1, Pallas kernels: none -> 117 us  [body(): pl.pallas_call(functools.partial(kernel, experts, half, part_p, chunk), o...]
    all_to_all x2 -> x0, blocking collectives: 107 us -> none  [the longest x1 89.9 us: copy_weights(): lax.all_to_all(chosen, 'expert', split_axis=1, concat_axis=1, tiled=True)]
    all_to_all x4 -> x0, waiting for transfers between devices: 96.2 us -> none  [the longest x1 89.4 us: copy_weights(): lax.all_to_all(stacked, 'expert', split_axis=1, concat_axis=1, tiled=True)]
    dot_general x13 -> x0, matrix products: 57.4 us -> none  [the longest x1 9.56 us: body(): jnp.einsum('nrcf,rdf->nrcd', grad_upv, ups, preferred_element_type=jnp.fl...]
    reshape x12 -> x0, local copies, waits for them, and re-layouts: 35.5 us -> none  [the longest x1 15.4 us: body(): all_rows = all_rows.reshape(ranks, 2, owned, width)]
    another operation x1 -> x0, local copies, waits for them, and re-layouts: 35.1 us -> none  [copy_weights(): stacked = jnp.stack([gate_w, up_w, down_w.T])]
    select_n x1 -> x0, local copies, waits for them, and re-layouts: 34.9 us -> none  [copy_weights(): chosen = jnp.take(pieces, copy_plan, axis=1).reshape(3, width, units)]
  transfers between devices with their start and end apart: 8 -> 0, of which waited for: 5 -> 0; matrix products, arithmetic and copies ran while one was open for 25% -> 0% of each run, Pallas kernels for 0% -> 0%
where the time goes in v1:
time: 138 us
  Pallas kernels  117 us (85%)
  local copies, waits for them, and re-layouts  16.1 us (12%)
  other arithmetic  3.84 us (3%)
    pallas_call x1, Pallas kernels, body(): pl.pallas_call(functools.partial(kernel, experts, half, part_p, chunk), o...  117 us
    unnamed x17, local copies, waits for them, and re-layouts  13.8 us

profile of v1, /device:TPU:1, one launch (start us, length us, event | category | flops | bytes accessed | tf_op | source)
XLA Modules:
  0.0 137.8 jit_solution(14075971349524449020)
XLA Ops:
  0.6 0.1 add.75
  0.7 0.1 add.76
  0.8 0.7 broadcast_multiply_fusion
  1.5 0.1 add.72
  1.6 0.7 fusion.4
  2.3 0.9 select_reduce_fusion
  3.2 0.1 add.83
  3.3 0.1 broadcast_in_dim.15
  3.4 0.1 add.78
  3.5 0.1 fusion.3
  3.6 0.9 constant_dynamic-update-slice_fusion.1
  4.5 0.9 constant_dynamic-update-slice_fusion
  5.4 0.7 pad_maximum_fusion.ext_ref
  6.2 117.2 %shard_map.143 = (bf16[2,16,3584]{2,1,0:T(8,128)(2,1)}, bf16[1,7168,128]{2,1,0:T(8,128)(2,1)}, bf16[1,7168,128]{2,1,0:T(8,128)(2,1)}, bf16[1,128,7168]{2,1,0:T(8...) custom-call(s32[8]{0:T(128)} %plan_ref.1, ...), custom_call_target="tpu_custom_call" | custom-call | flops 6000000000 | bytes 30000000 | tf_op jit(solution)/shard_map/pallas_call | solution.py:538
  123.3 0.9 slice_bitcast_fusion.1
  124.2 0.7 pad_maximum_fusion.3
  124.9 0.0 copy-start.4
  125.0 3.0 %copy.23 = bf16[1,7168,128]{2,1,0:T(8,128)(2,1)} copy(bf16[1,7168,128]{2,1,0:T(8,128)(2,1)} %get-tuple-element.47) | data formatting | bytes 3670016
  127.9 0.0 copy-done.4
  127.9 0.0 copy-start.3
  127.9 1.2 copy.24
  129.2 0.9 copy-done.3
  130.1 0.0 copy-start.2
  130.1 1.2 copy.25
  131.3 0.9 copy-done.2
  132.3 0.0 copy-start.1
  132.3 1.2 copy.26
  133.5 0.9 copy-done.1
  134.4 0.0 copy-start
  134.4 1.2 copy.27
  135.7 0.9 copy-done
  136.6 1.2 copy.28
  (11 shorter events, 0.1 us)
Async XLA Ops:
  124.9 3.0 %copy-start.4 = (bf16[1,7168,128]{2,1,0:T(8,128)(2,1)S(1)}, bf16[1,7168,128]{2,1,0:T(8,128)(2,1)}, u32[]{:S(2)}) copy-start(bf16[1,7168,128]{2,1,0:T(8,128)(2,1)} %get-tuple-element.48) | copy-start | bytes 5505028
  127.9 2.2 %copy-start.3 = (bf16[1,128,7168]{2,1,0:T(8,128)(2,1)S(1)}, bf16[1,128,7168]{2,1,0:T(8,128)(2,1)}, u32[]{:S(2)}) copy-start(bf16[1,128,7168]{2,1,0:T(8,128)(2,1)} %get-tuple-element.49) | copy-start | bytes 5505028
  130.1 2.2 %copy-start.2 = (bf16[1,7168,128]{2,1,0:T(8,128)(2,1)S(1)}, bf16[1,7168,128]{2,1,0:T(8,128)(2,1)}, u32[]{:S(2)}) copy-start(bf16[1,7168,128]{2,1,0:T(8,128)(2,1)} %get-tuple-element.50) | copy-start | bytes 5505028
  132.3 2.2 %copy-start.1 = (bf16[1,7168,128]{2,1,0:T(8,128)(2,1)S(1)}, bf16[1,7168,128]{2,1,0:T(8,128)(2,1)}, u32[]{:S(2)}) copy-start(bf16[1,7168,128]{2,1,0:T(8,128)(2,1)} %get-tuple-element.51) | copy-start | bytes 5505028
  134.4 2.2 %copy-start = (bf16[1,128,7168]{2,1,0:T(8,128)(2,1)S(1)}, bf16[1,128,7168]{2,1,0:T(8,128)(2,1)}, u32[]{:S(2)}) copy-start(bf16[1,128,7168]{2,1,0:T(8,128)(2,1)} %get-tuple-element.52) | copy-start | bytes 5505028

commit v2 on v1

--- a/solution.py
+++ b/solution.py
@@ -31,7 +31,10 @@
     part_p,
     chunk,
     plan_ref,
-    ext_ref,
+    assign_ref,
+    share_ref,
+    tok_ref,
+    cot_ref,
     w_gate,
     w_up,
     w_down,
@@ -42,9 +45,12 @@
     copy_gate_out,
     copy_up_out,
     copy_down_out,
+    ext,
     raw,
-    a2a_send,
-    a2a_recv,
+    own_send,
+    own_recv,
+    cpy_send,
+    cpy_recv,
     own,
     cpy,
     w1,
@@ -154,37 +160,94 @@
     greeted = [xp, xm, zp, sib] + [peer(i) for i in range(1, experts)]
     for dev in greeted:
         pl.semaphore_signal(barrier, inc=1, device_id=dev, device_id_type=MESH)
+
+    line = lax.broadcasted_iota(jnp.int32, (16, LANES), 0)
+    owned = jnp.zeros((16, LANES), jnp.int32)
+    copied = jnp.zeros((16, LANES), jnp.int32)
+    named = [assign_ref[t] for t in range(8)]
+    for t in range(8):
+        rank = jnp.int32(0)
+        for earlier in range(t):
+            rank += (named[earlier] == named[t]).astype(jnp.int32)
+        holder = jnp.int32(0)
+        for i in range(1, experts):
+            holder += i * (plan_ref[i] == named[t]).astype(jnp.int32)
+        spot = c * 2 + rank
+        aside = jnp.where(rank < share_ref[named[t]], holder * 16 + 8 + spot, -LANES)
+        here = line % 8 == t
+        owned = jnp.where(here, named[t] * 16 + spot, owned)
+        copied = jnp.where(here, aside, copied)
+    shift = (line // 8) * 4
+    lane = lax.broadcasted_iota(jnp.int32, (16, LANES), 1)
+    marks = jnp.logical_or(lane == owned + shift, lane == copied + shift).astype(F32).astype(BF16)
+
+    def stack(cols):
+        return jnp.concatenate(
+            [tok_ref[:, cols].astype(F32), cot_ref[:, cols].astype(F32)], axis=0
+        ).astype(BF16)
+
+    ext[:, :half] = stack(other_rows)
+    ext[:, half:] = marks
+    raw[c, :, :half] = stack(my_rows)
+    raw[c, :, half:] = marks
     pl.semaphore_wait(barrier, len(greeted))
 
     k_raw = fresh()
-    msg(k_raw, ext_ref.at[o], raw.at[c], sib)
+    msg(k_raw, ext, raw.at[c], sib)
     k_w = [fresh() for _ in range(3)]
     msg(k_w[0], w_gate.at[0, other_rows, :], w1.at[1, :, pl.ds(0, units)], sib)
     msg(k_w[1], w_up.at[0, other_rows, :], w1.at[1, :, pl.ds(units, units)], sib)
     msg(k_w[2], w_down.at[0, :, other_rows], wd.at[pl.ds(units, units), :], sib)
-    raw[c] = ext_ref[c]
     got(k_raw, raw.at[o], sib)
 
-    placed = raw[:, :, half:full].reshape(32, LANES)[:, : 16 * experts]
-    rows = raw[...].reshape(32, full)
-    a2a_send[...] = dot_tn(placed, rows).astype(BF16).reshape(experts, 16, full)
-    k_a2a = [fresh() for _ in range(experts - 1)]
+    size = 16 * experts
+    quarter = half // 2
+    spots = raw[:, :, half:full].reshape(32, LANES)[:, :size].astype(F32)
+    lane = lax.broadcasted_iota(jnp.int32, (32, size), 1)
+    own_spots = jnp.where((lane // 8) % 2 == 0, spots, 0.0)
+    cpy_spots = jnp.where((lane // 8) % 2 == 1, spots, 0.0)
+    left = raw[:, :, :quarter].reshape(32, quarter)
+    right = raw[:, :, quarter:half].reshape(32, quarter)
+    own_left = own_spots.astype(BF16)
+    own_right = pltpu.roll(own_spots, 8, 1).astype(BF16)
+    cpy_left = pltpu.roll(cpy_spots, size - 8, 1).astype(BF16)
+    cpy_right = cpy_spots.astype(BF16)
+
+    def spread(buf, first, second):
+        buf[:, :, :quarter] = (
+            (dot_tn(first, left) + dot_tn(second, right)).astype(BF16).reshape(experts, 16, quarter)
+        )
+
+    spread(own_send, own_left, own_right)
+    own_send[:, :, quarter:] = (
+        dot_tn(own_left, raw[:, :, half:full].reshape(32, LANES))
+        .astype(BF16)
+        .reshape(experts, 16, LANES)
+    )
+    k_own = [fresh() for _ in range(experts - 1)]
     for i in range(1, experts):
         dev = peer(i)
-        msg(k_a2a[i - 1], a2a_send.at[dev[1]], a2a_recv.at[ex], dev)
-    a2a_recv[ex] = a2a_send[ex]
-    for i in range(1, experts):
-        got(k_a2a[i - 1], a2a_recv.at[lax.rem(ex + experts - i, experts)], peer(i))
-
-    size = 16 * experts
-    to = lax.broadcasted_iota(jnp.int32, (size, size), 0)
-    fr = lax.broadcasted_iota(jnp.int32, (size, size), 1)
-    want = (
-        ((fr // 8) % 2) * block + ((fr // 4) % 2) * per_chip + (fr // 16) * 4 + fr % 4
-    )
-    moved = dot((to == want).astype(BF16), a2a_recv[...].reshape(size, full)).astype(BF16)
-    own[me] = moved[:block]
-    cpy[me] = moved[block:, :half]
+        msg(k_own[i - 1], own_send.at[dev[1]], own_recv.at[ex], dev)
+    own_recv[ex] = own_send[ex]
+    spread(cpy_send, cpy_left, cpy_right)
+    k_cpy = [fresh() for _ in range(experts - 1)]
+    for i in range(1, experts):
+        dev = peer(i)
+        msg(k_cpy[i - 1], cpy_send.at[dev[1]], cpy_recv.at[ex], dev)
+    cpy_recv[ex] = cpy_send[ex]
+
+    to = lax.broadcasted_iota(jnp.int32, (block, size), 0)
+    fr = lax.broadcasted_iota(jnp.int32, (block, size), 1)
+    match = to == ((fr // 4) % 2) * per_chip + (fr // 16) * 4 + fr % 4
+    take_left = jnp.logical_and(match, (fr // 8) % 2 == 0).astype(BF16)
+    take_right = jnp.logical_and(match, (fr // 8) % 2 == 1).astype(BF16)
+
+    for i in range(1, experts):
+        got(k_own[i - 1], own_recv.at[lax.rem(ex + experts - i, experts)], peer(i))
+    arrived = own_recv[...].reshape(size, quarter + LANES)
+    own[me, :, :quarter] = dot(take_left, arrived[:, :quarter]).astype(BF16)
+    own[me, :, quarter:half] = dot(take_right, arrived[:, :quarter]).astype(BF16)
+    own[me, :, half:] = dot(take_left, arrived[:, quarter:]).astype(BF16)
 
     def gather(buf, width):
         keys = [fresh() for _ in range(18)]
@@ -248,6 +311,11 @@
     own_first()
     own_second()
     own_third()
+    for i in range(1, experts):
+        got(k_cpy[i - 1], cpy_recv.at[lax.rem(ex + experts - i, experts)], peer(i))
+    arrived = cpy_recv[...].reshape(size, quarter)
+    cpy[me, :, :quarter] = dot(take_left, arrived).astype(BF16)
+    cpy[me, :, quarter:] = dot(take_right, arrived).astype(BF16)
     cpy_first()
 
     for load in weight_loads:
@@ -424,6 +492,15 @@
     k_gsib = fresh()
     msg(k_gsib, gx2.at[0], gx2.at[1], sib)
 
+    got(k_gsib, gx2.at[1], sib)
+    for i in range(2):
+        gcat[:, 2 * units * i : 2 * units * (i + 1)] = gx2[i, :, :, units:].reshape(
+            slots, 2 * units
+        )
+        hcat[:, units * i : units * (i + 1)] = gx2[i, :, :, :units].reshape(slots, units)
+    weight_grads(cpy, ct1, ct2)
+    finish_cpy = write_grads(ct1, ct2, copy_gate_out, copy_up_out, copy_down_out)
+
     got(k_z[0], rz.at[0], zp)
     got(k_xf[0], rxf.at[0], xm)
     got(k_xf[1], rxf.at[1], xp)
@@ -447,7 +524,6 @@
     fr = lax.broadcasted_iota(jnp.int32, (size, block), 1)
     want = (to // 16) * 4 + ((to // 4) % 2) * per_chip + to % 4
     side = (to // 8) % 2
-    quarter = half // 2
     back_send[...] = (
         dot(jnp.logical_and(fr == want, side == 0).astype(BF16), fin[:, :quarter])
         + dot(jnp.logical_and(fr == want, side == 1).astype(BF16), fin[:, quarter:])
@@ -458,28 +534,11 @@
         msg(k_back[i - 1], back_send.at[dev[1]], back_recv.at[ex], dev)
     back_recv[ex] = back_send[ex]
 
-    got(k_gsib, gx2.at[1], sib)
-    for i in range(2):
-        gcat[:, 2 * units * i : 2 * units * (i + 1)] = gx2[i, :, :, units:].reshape(
-            slots, 2 * units
-        )
-        hcat[:, units * i : units * (i + 1)] = gx2[i, :, :, :units].reshape(slots, units)
-    weight_grads(cpy, ct1, ct2)
-    finish_cpy = write_grads(ct1, ct2, copy_gate_out, copy_up_out, copy_down_out)
-
     for i in range(1, experts):
         got(k_back[i - 1], back_recv.at[lax.rem(ex + experts - i, experts)], peer(i))
-    spots = raw[:, :, half:full].reshape(32, LANES).astype(F32)
-    lane = lax.broadcasted_iota(jnp.int32, (32, LANES), 1)
-    spots = jnp.where((lane // 8) % 2 == 0, spots, 0.0)
-    later = pltpu.roll(spots, 8, 1)
     got_back = back_recv[...].reshape(size, quarter)
-    outs[:, :, :quarter] = (
-        dot(spots[:, :size].astype(BF16), got_back).astype(BF16).reshape(2, 16, quarter)
-    )
-    outs[:, :, quarter:] = (
-        dot(later[:, :size].astype(BF16), got_back).astype(BF16).reshape(2, 16, quarter)
-    )
+    outs[:, :, :quarter] = dot(own_left, got_back).astype(BF16).reshape(2, 16, quarter)
+    outs[:, :, quarter:] = dot(own_right, got_back).astype(BF16).reshape(2, 16, quarter)
     k_out = fresh()
     msg(k_out, outs.at[o], o_out.at[c], sib)
     mine_out = local(outs.at[c], o_out.at[c])
@@ -491,24 +550,18 @@
         copy.wait_send()
 
 
-def placing(assign, copy_share, copy_plan, experts):
-    expert_of = assign[:, 0]
-    numbers = jnp.arange(experts, dtype=jnp.int32)
-    onehot = (expert_of[:, None] == numbers[None, :]).astype(jnp.int32)
-    before = jnp.cumsum(onehot, axis=0) - onehot
-    rank_in = jnp.sum(before * onehot, axis=1)
-    limit_rows = jnp.sum(copy_share[0][None, :] * onehot, axis=1)
-    holder = jnp.sum(
-        numbers[None, :] * (copy_plan[None, :] == expert_of[:, None]).astype(jnp.int32), axis=1
-    )
-    core = lax.rem(lax.axis_index("dp"), 2)
-    array = jnp.arange(2, dtype=jnp.int32)[:, None]
-    spot = array * 4 + core * 2 + rank_in[None, :]
-    owned = expert_of[None, :] * 16 + spot
-    copied = jnp.where((rank_in < limit_rows)[None, :], holder[None, :] * 16 + 8 + spot, -1)
-    places = jnp.arange(LANES, dtype=jnp.int32)
-    hit = jnp.logical_or(places == owned[:, :, None], places == copied[:, :, None])
-    return hit.astype(BF16).reshape(-1, LANES)
+def finish(o, g, u, d, cg, cu, cd, mixed, grad_in, g_out, u_out, d_out, cg_out, cu_out, cd_out, sem):
+    copies = []
+    pairs = ((g, g_out), (u, u_out), (d, d_out), (cg, cg_out), (cu, cu_out), (cd, cd_out))
+    for i, (src, dst) in enumerate(pairs):
+        copies.append(pltpu.make_async_copy(src, dst, sem.at[i]))
+        copies[-1].start()
+    half = o.shape[2]
+    for side in range(2):
+        mixed[:, half * side : half * (side + 1)] = o[side, :8, :]
+        grad_in[:, half * side : half * (side + 1)] = o[side, 8:, :]
+    for copy in copies:
+        copy.wait()
 
 
 def body(tokens, assign, copy_share, copy_plan, grad_out, w_gate, w_up, w_down):
@@ -523,18 +576,12 @@
     slots = 8 * per_chip
     block = 2 * per_chip
     mid = block // 2
-    marks = placing(assign, copy_share, copy_plan, experts)
-    both = jnp.concatenate([tokens, grad_out], axis=0)
-    ext = jnp.stack(
-        [
-            jnp.concatenate([both[:, :half], marks], axis=1),
-            jnp.concatenate([both[:, half:], marks], axis=1),
-        ]
-    )
     vmem = pltpu.VMEM
     part_q = half - part_p
     messages = 128
     any_spec = pl.BlockSpec(memory_space=pl.ANY)
+    smem_spec = pl.BlockSpec(memory_space=pltpu.SMEM)
+    vmem_spec = pl.BlockSpec(memory_space=pltpu.VMEM)
     o, g, u, d, cg, cu, cd = pl.pallas_call(
         functools.partial(kernel, experts, half, part_p, chunk),
         out_shape=[
@@ -547,17 +594,23 @@
             jax.ShapeDtypeStruct(w_down.shape, BF16),
         ],
         in_specs=[
-            pl.BlockSpec(memory_space=pltpu.SMEM),
-            pl.BlockSpec(memory_space=pltpu.VMEM),
+            smem_spec,
+            smem_spec,
+            smem_spec,
+            vmem_spec,
+            vmem_spec,
             any_spec,
             any_spec,
             any_spec,
         ],
         out_specs=[any_spec] * 7,
         scratch_shapes=[
+            vmem((16, full), BF16),
             vmem((2, 16, full), BF16),
-            vmem((experts, 16, full), BF16),
-            vmem((experts, 16, full), BF16),
+            vmem((experts, 16, half // 2 + LANES), BF16),
+            vmem((experts, 16, half // 2 + LANES), BF16),
+            vmem((experts, 16, half // 2), BF16),
+            vmem((experts, 16, half // 2), BF16),
             vmem((8, block, full), BF16),
             vmem((8, block, half), BF16),
             vmem((2, half, 2 * units), BF16),
@@ -592,15 +645,38 @@
         compiler_params=pltpu.CompilerParams(
             collective_id=0,
             has_side_effects=True,
-            vmem_limit_bytes=56 * 1024 * 1024,
+            vmem_limit_bytes=42 * 1024 * 1024,
         ),
         cost_estimate=pl.CostEstimate(
             flops=6_000_000_000, bytes_accessed=30_000_000, transcendentals=32768
         ),
-    )(copy_plan, ext, w_gate, w_up, w_down)
-    mixed = jnp.concatenate([o[0, :rows_in], o[1, :rows_in]], axis=1)
-    grad_in = jnp.concatenate([o[0, rows_in:], o[1, rows_in:]], axis=1)
-    return (mixed, grad_in, g, u, d, cg, cu, cd)
+    )(
+        copy_plan,
+        assign.reshape(rows_in),
+        copy_share.reshape(experts),
+        tokens,
+        grad_out,
+        w_gate,
+        w_up,
+        w_down,
+    )
+    return pl.pallas_call(
+        finish,
+        out_shape=[
+            jax.ShapeDtypeStruct(tokens.shape, BF16),
+            jax.ShapeDtypeStruct(tokens.shape, BF16),
+            jax.ShapeDtypeStruct(w_gate.shape, BF16),
+            jax.ShapeDtypeStruct(w_up.shape, BF16),
+            jax.ShapeDtypeStruct(w_down.shape, BF16),
+            jax.ShapeDtypeStruct(w_gate.shape, BF16),
+            jax.ShapeDtypeStruct(w_up.shape, BF16),
+            jax.ShapeDtypeStruct(w_down.shape, BF16),
+        ],
+        in_specs=[vmem_spec] + [any_spec] * 6,
+        out_specs=[vmem_spec] * 2 + [any_spec] * 6,
+        scratch_shapes=[pltpu.SemaphoreType.DMA((6,))],
+        compiler_params=pltpu.CompilerParams(vmem_limit_bytes=4 * 1024 * 1024),
+    )(o, g, u, d, cg, cu, cd)
 
 
 def solution(mesh):

time: 138 us -> 119 us (0.86)
  local copies, waits for them, and re-layouts: 16.1 us -> 3.75 us
  other arithmetic: 3.84 us -> 0 us
  Pallas kernels: 117 us -> 114 us
    unnamed x17 -> x10, local copies, waits for them, and re-layouts: 13.8 us -> 3.75 us
    pallas_call x1, Pallas kernels: 117 us -> 110 us  [body(): pl.pallas_call(functools.partial(kernel, experts, half, part_p, chunk), o...]
    pallas_call x0 -> x1, Pallas kernels: none -> 4.88 us  [body(): pl.pallas_call(finish, out_shape=[jax.ShapeDtypeStruct(tokens.shape, BF16...]
where the time goes in v2:
time: 119 us
  Pallas kernels  114 us (96%)
  local copies, waits for them, and re-layouts  3.75 us (3%)
    pallas_call x1, Pallas kernels, body(): pl.pallas_call(functools.partial(kernel, experts, half, part_p, chunk), o...  110 us
    pallas_call x1, Pallas kernels, body(): pl.pallas_call(finish, out_shape=[jax.ShapeDtypeStruct(tokens.shape, BF16...  4.88 us
    unnamed x10, local copies, waits for them, and re-layouts  3.75 us

profile of v2, /device:TPU:1, one launch (start us, length us, event | category | flops | bytes accessed | tf_op | source)
XLA Modules:
  0.0 118.8 jit_solution(10876817654216915482)
XLA Ops:
  0.6 0.0 copy-start
  0.6 0.9 copy-done
  1.5 0.0 copy-start.1
  1.5 0.9 copy-done.1
  2.4 0.0 copy-start.2
  2.4 0.7 copy-done.2
  3.1 0.0 copy-start.3
  3.1 0.7 copy-done.3
  3.7 0.0 copy-start.4
  3.7 0.7 copy-done.4
  4.4 109.5 %shard_map.143 = (bf16[2,16,3584]{2,1,0:T(8,128)(2,1)S(1)}, bf16[1,7168,128]{2,1,0:T(8,128)(2,1)S(1)}, bf16[1,7168,128]{2,1,0:T(8,128)(2,1)S(1)}, bf16[1,128,716...) custom-call(s32[8]{0:T(128)S(1)} %copy-done.2, ...), custom_call_target="tpu_custom_call" | custom-call | flops 6000000000 | bytes 30000000 | tf_op jit(solution)/shard_map/pallas_call | solution.py:585
  113.9 4.9 %shard_map.144 = (bf16[8,7168]{1,0:T(8,128)(2,1)}, bf16[8,7168]{1,0:T(8,128)(2,1)}, bf16[1,7168,128]{2,1,0:T(8,128)(2,1)}, bf16[1,7168,128]{2,1,0:T(8,128)(2,1)}...) custom-call(bf16[2,16,3584]{2,1,0:T(8,128)(2,1)S(1)} %get-tuple-elem, ...), custom_call_target="tpu_custom_call" | custom-call | tf_op jit(solution)/shard_map/pallas_call | solution.py:663
Async XLA Ops:
  0.6 0.9 copy-start
  1.5 0.9 copy-start.1
  2.4 0.7 copy-start.2
  3.1 0.7 copy-start.3
  3.7 0.7 copy-start.4

commit v3 on v2

--- a/solution.py
+++ b/solution.py
@@ -29,12 +29,11 @@
     experts,
     half,
     part_p,
+    sum_p,
     chunk,
-    plan_ref,
-    assign_ref,
-    share_ref,
-    tok_ref,
-    cot_ref,
+    ints_in,
+    tok_in,
+    cot_in,
     w_gate,
     w_up,
     w_down,
@@ -45,10 +44,15 @@
     copy_gate_out,
     copy_up_out,
     copy_down_out,
+    ints,
+    tok_ref,
+    cot_ref,
     ext,
     raw,
-    own_send,
-    own_recv,
+    own_send_p,
+    own_recv_p,
+    own_send_q,
+    own_recv_q,
     cpy_send,
     cpy_recv,
     own,
@@ -71,8 +75,10 @@
     rf_q,
     rzq,
     fin,
-    back_send,
-    back_recv,
+    back_send_p,
+    back_recv_p,
+    back_send_q,
+    back_recv_q,
     outs,
     st1,
     st2,
@@ -89,7 +95,7 @@
     block = 2 * per_chip
     mid = block // 2
     steps = half // chunk
-    part_q = half - part_p
+    sum_q = half - sum_p
 
     dp = lax.axis_index("dp")
     ex = lax.axis_index("expert")
@@ -150,30 +156,39 @@
     my_rows = pl.ds(pl.multiple_of(c * half, half), half)
     other_rows = pl.ds(pl.multiple_of(o * half, half), half)
 
+    first_loads = [
+        local(ints_in, ints),
+        local(tok_in, tok_ref),
+        local(cot_in, cot_ref),
+    ]
+
+    barrier = pltpu.get_barrier_semaphore()
+    greeted = [xp, xm, zp, sib] + [peer(i) for i in range(1, experts)]
+    for dev in greeted:
+        pl.semaphore_signal(barrier, inc=1, device_id=dev, device_id_type=MESH)
+
     weight_loads = [
         local(w_gate.at[0, my_rows, :], w1.at[0, :, pl.ds(0, units)]),
         local(w_up.at[0, my_rows, :], w1.at[0, :, pl.ds(units, units)]),
         local(w_down.at[0, :, my_rows], wd.at[pl.ds(0, units), :]),
     ]
 
-    barrier = pltpu.get_barrier_semaphore()
-    greeted = [xp, xm, zp, sib] + [peer(i) for i in range(1, experts)]
-    for dev in greeted:
-        pl.semaphore_signal(barrier, inc=1, device_id=dev, device_id_type=MESH)
+    for load in first_loads:
+        load.wait()
 
     line = lax.broadcasted_iota(jnp.int32, (16, LANES), 0)
     owned = jnp.zeros((16, LANES), jnp.int32)
     copied = jnp.zeros((16, LANES), jnp.int32)
-    named = [assign_ref[t] for t in range(8)]
+    named = [ints[experts + t] for t in range(8)]
     for t in range(8):
         rank = jnp.int32(0)
         for earlier in range(t):
             rank += (named[earlier] == named[t]).astype(jnp.int32)
         holder = jnp.int32(0)
         for i in range(1, experts):
-            holder += i * (plan_ref[i] == named[t]).astype(jnp.int32)
+            holder += i * (ints[i] == named[t]).astype(jnp.int32)
         spot = c * 2 + rank
-        aside = jnp.where(rank < share_ref[named[t]], holder * 16 + 8 + spot, -LANES)
+        aside = jnp.where(rank < ints[experts + 8 + named[t]], holder * 16 + 8 + spot, -LANES)
         here = line % 8 == t
         owned = jnp.where(here, named[t] * 16 + spot, owned)
         copied = jnp.where(here, aside, copied)
@@ -201,40 +216,47 @@
     got(k_raw, raw.at[o], sib)
 
     size = 16 * experts
-    quarter = half // 2
     spots = raw[:, :, half:full].reshape(32, LANES)[:, :size].astype(F32)
     lane = lax.broadcasted_iota(jnp.int32, (32, size), 1)
     own_spots = jnp.where((lane // 8) % 2 == 0, spots, 0.0)
     cpy_spots = jnp.where((lane // 8) % 2 == 1, spots, 0.0)
-    left = raw[:, :, :quarter].reshape(32, quarter)
-    right = raw[:, :, quarter:half].reshape(32, quarter)
     own_left = own_spots.astype(BF16)
     own_right = pltpu.roll(own_spots, 8, 1).astype(BF16)
     cpy_left = pltpu.roll(cpy_spots, size - 8, 1).astype(BF16)
     cpy_right = cpy_spots.astype(BF16)
 
-    def spread(buf, first, second):
-        buf[:, :, :quarter] = (
-            (dot_tn(first, left) + dot_tn(second, right)).astype(BF16).reshape(experts, 16, quarter)
-        )
-
-    spread(own_send, own_left, own_right)
-    own_send[:, :, quarter:] = (
+    def spread(first, second, start, count):
+        middle = start + count // 2
+        left = raw[:, :, start:middle].reshape(32, count // 2)
+        right = raw[:, :, middle : start + count].reshape(32, count // 2)
+        both = dot_tn(first, left) + dot_tn(second, right)
+        return both.astype(BF16).reshape(experts, 16, count // 2)
+
+    def exchange(source, target):
+        keys = [fresh() for _ in range(experts - 1)]
+        for i in range(1, experts):
+            dev = peer(i)
+            msg(keys[i - 1], source.at[dev[1]], target.at[ex], dev)
+        target[ex] = source[ex]
+
+        def arrive():
+            for i in range(1, experts):
+                got(keys[i - 1], target.at[lax.rem(ex + experts - i, experts)], peer(i))
+
+        return arrive
+
+    side_q = (half - part_p) // 2
+    own_send_p[...] = spread(own_left, own_right, 0, part_p)
+    arrive_p = exchange(own_send_p, own_recv_p)
+    own_send_q[:, :, :side_q] = spread(own_left, own_right, part_p, half - part_p)
+    own_send_q[:, :, side_q:] = (
         dot_tn(own_left, raw[:, :, half:full].reshape(32, LANES))
         .astype(BF16)
         .reshape(experts, 16, LANES)
     )
-    k_own = [fresh() for _ in range(experts - 1)]
-    for i in range(1, experts):
-        dev = peer(i)
-        msg(k_own[i - 1], own_send.at[dev[1]], own_recv.at[ex], dev)
-    own_recv[ex] = own_send[ex]
-    spread(cpy_send, cpy_left, cpy_right)
-    k_cpy = [fresh() for _ in range(experts - 1)]
-    for i in range(1, experts):
-        dev = peer(i)
-        msg(k_cpy[i - 1], cpy_send.at[dev[1]], cpy_recv.at[ex], dev)
-    cpy_recv[ex] = cpy_send[ex]
+    arrive_q = exchange(own_send_q, own_recv_q)
+    cpy_send[...] = spread(cpy_left, cpy_right, 0, half)
+    arrive_cpy = exchange(cpy_send, cpy_recv)
 
     to = lax.broadcasted_iota(jnp.int32, (block, size), 0)
     fr = lax.broadcasted_iota(jnp.int32, (block, size), 1)
@@ -242,12 +264,11 @@
     take_left = jnp.logical_and(match, (fr // 8) % 2 == 0).astype(BF16)
     take_right = jnp.logical_and(match, (fr // 8) % 2 == 1).astype(BF16)
 
-    for i in range(1, experts):
-        got(k_own[i - 1], own_recv.at[lax.rem(ex + experts - i, experts)], peer(i))
-    arrived = own_recv[...].reshape(size, quarter + LANES)
-    own[me, :, :quarter] = dot(take_left, arrived[:, :quarter]).astype(BF16)
-    own[me, :, quarter:half] = dot(take_right, arrived[:, :quarter]).astype(BF16)
-    own[me, :, half:] = dot(take_left, arrived[:, quarter:]).astype(BF16)
+    def collect(buf, arrived, start, count):
+        middle = start + count // 2
+        rows = arrived[:, :, : count // 2].reshape(size, count // 2)
+        buf[me, :, start:middle] = dot(take_left, rows).astype(BF16)
+        buf[me, :, middle : start + count] = dot(take_right, rows).astype(BF16)
 
     def gather(buf, width):
         keys = [fresh() for _ in range(18)]
@@ -260,24 +281,26 @@
 
         y = 1 - z
 
-        def first():
-            msg(keys[9], cut(me, 1), cut(me, 1), zp)
+        def first_p():
             msg(keys[0], cut(me, 0), cut(me, 0), xp)
             msg(keys[1], cut(me, 0), cut(me, 0), xm)
-            msg(keys[2], cut(me, 0), cut(me, 0), zp)
+
+        def first_q():
+            msg(keys[9], cut(me, 1), cut(me, 1), zp)
             msg(keys[10], cut(me, 1), cut(me, 1), xp)
             msg(keys[11], cut(me, 1), cut(me, 1), xm)
 
         def second():
-            got(keys[9], cut(chip(0, y), 1), zp)
-            msg(keys[12], cut(chip(0, y), 1), cut(chip(0, y), 1), xp)
-            msg(keys[13], cut(chip(0, y), 1), cut(chip(0, y), 1), xm)
             got(keys[0], cut(chip(3, z), 0), xm)
             msg(keys[3], cut(chip(3, z), 0, 0), cut(chip(3, z), 0, 0), xp)
             msg(keys[5], cut(chip(3, z), 0), cut(chip(3, z), 0), zp)
             got(keys[1], cut(chip(1, z), 0), xp)
             msg(keys[4], cut(chip(1, z), 0, 1), cut(chip(1, z), 0, 1), xm)
             msg(keys[6], cut(chip(1, z), 0), cut(chip(1, z), 0), zp)
+            got(keys[9], cut(chip(0, y), 1), zp)
+            msg(keys[12], cut(chip(0, y), 1), cut(chip(0, y), 1), xp)
+            msg(keys[13], cut(chip(0, y), 1), cut(chip(0, y), 1), xm)
+            msg(keys[2], cut(me, 0), cut(me, 0), zp)
 
         def third():
             got(keys[10], cut(chip(3, z), 1), xm)
@@ -304,19 +327,23 @@
             got(keys[16], cut(chip(2, y), 1, 0), xm)
             got(keys[17], cut(chip(2, y), 1, 1), xp)
 
-        return first, second, third, last
-
-    own_first, own_second, own_third, own_last = gather(own, full)
-    cpy_first, cpy_second, cpy_third, cpy_last = gather(cpy, half)
-    own_first()
+        return first_p, first_q, second, third, last
+
+    own_first_p, own_first_q, own_second, own_third, own_last = gather(own, full)
+    cpy_first_p, cpy_first_q, cpy_second, cpy_third, cpy_last = gather(cpy, half)
+    arrive_p()
+    collect(own, own_recv_p, 0, part_p)
+    own_first_p()
+    arrive_q()
+    collect(own, own_recv_q, part_p, half - part_p)
+    own[me, :, half:] = dot(take_left, own_recv_q[:, :, side_q:].reshape(size, LANES)).astype(BF16)
+    own_first_q()
     own_second()
     own_third()
-    for i in range(1, experts):
-        got(k_cpy[i - 1], cpy_recv.at[lax.rem(ex + experts - i, experts)], peer(i))
-    arrived = cpy_recv[...].reshape(size, quarter)
-    cpy[me, :, :quarter] = dot(take_left, arrived).astype(BF16)
-    cpy[me, :, quarter:] = dot(take_right, arrived).astype(BF16)
-    cpy_first()
+    arrive_cpy()
+    collect(cpy, cpy_recv, 0, half)
+    cpy_first_p()
+    cpy_first_q()
 
     for load in weight_loads:
         load.wait()
@@ -325,27 +352,19 @@
     got(k_w[2], wd.at[pl.ds(units, units), :], sib)
     own_last()
 
-    pre[...] = jnp.zeros_like(pre)
-
     def tokens_of(buf, cols):
-        return buf[:, :per_chip, cols].reshape(slots, chunk)
+        return buf[:, :per_chip, cols].reshape(slots, -1)
 
     def backs_of(buf, cols):
-        return buf[:, per_chip:, cols].reshape(slots, chunk)
-
-    @pl.loop(0, steps)
-    def _(step):
-        cols = pl.ds(pl.multiple_of(step * chunk, chunk), chunk)
-        t = tokens_of(own, cols)
-        g = backs_of(own, cols)
-        pre[0, :, : 2 * units] += dot(t, w1[0, cols, :])
-        pre[1, :, : 2 * units] += dot(t, w1[1, cols, :])
-        gh = dot_nt(g, wd[:, cols])
-        pre[0, :, 2 * units :] += gh[:, :units]
-        pre[1, :, 2 * units :] += gh[:, units:]
-
+        return buf[:, per_chip:, cols].reshape(slots, -1)
+
+    pre[1, :, : 2 * units] = dot(tokens_of(own, slice(0, half)), w1[1])
+    gh = dot_nt(backs_of(own, slice(0, half)), wd[...])
+    pre[1, :, 2 * units :] = gh[:, units:]
     k_pre = fresh()
     msg(k_pre, pre.at[1], pre_recv, sib)
+    pre[0, :, : 2 * units] = dot(tokens_of(own, slice(0, half)), w1[0])
+    pre[0, :, 2 * units :] = gh[:, :units]
     cpy_second()
     got(k_pre, pre_recv, sib)
     total = pre[0] + pre_recv[...]
@@ -381,8 +400,8 @@
         r = dot_nt(acts[0, :, units:], w1[0, cols, :]) + dot_nt(acts[1, :, units:], w1[1, cols, :])
         part[:, per_chip:, cols] = r.astype(BF16).reshape(8, per_chip, chunk)
 
-    cols_p = pl.ds(0, part_p)
-    cols_q = pl.ds(part_p, part_q)
+    cols_p = pl.ds(0, sum_p)
+    cols_q = pl.ds(sum_p, sum_q)
     first_rows = pl.ds(0, mid)
     last_rows = pl.ds(mid, mid)
     every = pl.ds(0, block)
@@ -408,7 +427,7 @@
     for i in range(1, experts):
         got(k_gx1[i - 1], gx1.at[lax.rem(ex + experts - i, experts)], peer(i))
     for i in range(experts):
-        gx2s[i] = gx1[plan_ref[i]]
+        gx2s[i] = gx1[ints[i]]
     k_gx2 = [fresh() for _ in range(experts - 1)]
     for i in range(1, experts):
         dev = peer(i)
@@ -456,13 +475,15 @@
     weight_grads(own, st1, st2)
     finish_own = write_grads(st1, st2, gate_out, up_out, down_out)
 
-    for i, zz in enumerate((y, z)):
+    def pass_on(i, zz):
         got(k_yo[i][0], ro_q.at[i, 0], xm)
         add(part.at[chip(1, zz), first_rows, cols_q], ro_q.at[i, 0])
         msg(k_yf[i][0], part.at[chip(1, zz), every, cols_q], rf_q.at[i, 0], xp)
         got(k_yo[i][1], ro_q.at[i, 1], xp)
         add(part.at[chip(3, zz), last_rows, cols_q], ro_q.at[i, 1])
         msg(k_yf[i][1], part.at[chip(3, zz), every, cols_q], rf_q.at[i, 1], xm)
+
+    pass_on(0, y)
     got(k_z[2], rz.at[2], zp)
     add(part.at[chip(2, z), every, cols_p], rz.at[2])
     msg(k_xo[0], part.at[chip(2, z), first_rows, cols_p], rxo.at[0], xp)
@@ -471,6 +492,7 @@
     add(part.at[chip(1, z), every, cols_p], rz.at[1])
     got(k_z[3], rz.at[3], zp)
     add(part.at[chip(3, z), every, cols_p], rz.at[3])
+    pass_on(1, z)
     got(k_xo[0], rxo.at[0], xm)
     add(part.at[chip(1, z), first_rows, cols_p], rxo.at[0])
     msg(k_xf[0], part.at[chip(1, z), every, cols_p], rxf.at[0], xp)
@@ -501,6 +523,28 @@
     weight_grads(cpy, ct1, ct2)
     finish_cpy = write_grads(ct1, ct2, copy_gate_out, copy_up_out, copy_down_out)
 
+    to = lax.broadcasted_iota(jnp.int32, (size, block), 0)
+    fr = lax.broadcasted_iota(jnp.int32, (size, block), 1)
+    match = fr == (to // 16) * 4 + ((to // 4) % 2) * per_chip + to % 4
+    put_left = jnp.logical_and(match, (to // 8) % 2 == 0).astype(BF16)
+    put_right = jnp.logical_and(match, (to // 8) % 2 == 1).astype(BF16)
+
+    def pack(start, count):
+        middle = start + count // 2
+        both = dot(put_left, fin[:, start:middle]) + dot(put_right, fin[:, middle : start + count])
+        return both.astype(BF16).reshape(experts, 16, count // 2)
+
+    got(k_yf[1][0], rf_q.at[1, 0], xm)
+    got(k_yf[1][1], rf_q.at[1, 1], xp)
+    got(k_w0, rzq, zp)
+    fin[:, cols_q] = (
+        part[me, :, cols_q].astype(F32)
+        + rf_q[1, 0].astype(F32)
+        + rf_q[1, 1].astype(F32)
+        + rzq[...].astype(F32)
+    ).astype(BF16)
+    back_send_q[...] = pack(sum_p, sum_q)
+    back_q = exchange(back_send_q, back_recv_q)
     got(k_z[0], rz.at[0], zp)
     got(k_xf[0], rxf.at[0], xm)
     got(k_xf[1], rxf.at[1], xp)
@@ -510,35 +554,21 @@
         + rxf[0].astype(F32)
         + rxf[1].astype(F32)
     ).astype(BF16)
-    got(k_yf[1][0], rf_q.at[1, 0], xm)
-    got(k_yf[1][1], rf_q.at[1, 1], xp)
-    got(k_w0, rzq, zp)
-    fin[:, cols_q] = (
-        part[me, :, cols_q].astype(F32)
-        + rf_q[1, 0].astype(F32)
-        + rf_q[1, 1].astype(F32)
-        + rzq[...].astype(F32)
-    ).astype(BF16)
-
-    to = lax.broadcasted_iota(jnp.int32, (size, block), 0)
-    fr = lax.broadcasted_iota(jnp.int32, (size, block), 1)
-    want = (to // 16) * 4 + ((to // 4) % 2) * per_chip + to % 4
-    side = (to // 8) % 2
-    back_send[...] = (
-        dot(jnp.logical_and(fr == want, side == 0).astype(BF16), fin[:, :quarter])
-        + dot(jnp.logical_and(fr == want, side == 1).astype(BF16), fin[:, quarter:])
-    ).astype(BF16).reshape(experts, 16, quarter)
-    k_back = [fresh() for _ in range(experts - 1)]
-    for i in range(1, experts):
-        dev = peer(i)
-        msg(k_back[i - 1], back_send.at[dev[1]], back_recv.at[ex], dev)
-    back_recv[ex] = back_send[ex]
-
-    for i in range(1, experts):
-        got(k_back[i - 1], back_recv.at[lax.rem(ex + experts - i, experts)], peer(i))
-    got_back = back_recv[...].reshape(size, quarter)
-    outs[:, :, :quarter] = dot(own_left, got_back).astype(BF16).reshape(2, 16, quarter)
-    outs[:, :, quarter:] = dot(own_right, got_back).astype(BF16).reshape(2, 16, quarter)
+    back_send_p[...] = pack(0, sum_p)
+    back_p = exchange(back_send_p, back_recv_p)
+
+    def restore(buf, start, count):
+        middle = start + count // 2
+        rows = buf[...].reshape(size, count // 2)
+        outs[:, :, start:middle] = dot(own_left, rows).astype(BF16).reshape(2, 16, count // 2)
+        outs[:, :, middle : start + count] = (
+            dot(own_right, rows).astype(BF16).reshape(2, 16, count // 2)
+        )
+
+    back_q()
+    restore(back_recv_q, sum_p, sum_q)
+    back_p()
+    restore(back_recv_p, 0, sum_p)
     k_out = fresh()
     msg(k_out, outs.at[o], o_out.at[c], sib)
     mine_out = local(outs.at[c], o_out.at[c])
@@ -577,13 +607,13 @@
     block = 2 * per_chip
     mid = block // 2
     vmem = pltpu.VMEM
-    part_q = half - part_p
+    sum_p = 5 * (chunk // 2)
+    sum_q = half - sum_p
     messages = 128
     any_spec = pl.BlockSpec(memory_space=pl.ANY)
-    smem_spec = pl.BlockSpec(memory_space=pltpu.SMEM)
     vmem_spec = pl.BlockSpec(memory_space=pltpu.VMEM)
     o, g, u, d, cg, cu, cd = pl.pallas_call(
-        functools.partial(kernel, experts, half, part_p, chunk),
+        functools.partial(kernel, experts, half, part_p, sum_p, chunk),
         out_shape=[
             jax.ShapeDtypeStruct((2, 16, half), BF16),
             jax.ShapeDtypeStruct(w_gate.shape, BF16),
@@ -594,21 +624,24 @@
             jax.ShapeDtypeStruct(w_down.shape, BF16),
         ],
         in_specs=[
-            smem_spec,
-            smem_spec,
-            smem_spec,
-            vmem_spec,
-            vmem_spec,
+            any_spec,
+            any_spec,
+            any_spec,
             any_spec,
             any_spec,
             any_spec,
         ],
         out_specs=[any_spec] * 7,
         scratch_shapes=[
+            pltpu.SMEM((2 * experts + rows_in,), jnp.int32),
+            vmem((rows_in, width), BF16),
+            vmem((rows_in, width), BF16),
             vmem((16, full), BF16),
             vmem((2, 16, full), BF16),
-            vmem((experts, 16, half // 2 + LANES), BF16),
-            vmem((experts, 16, half // 2 + LANES), BF16),
+            vmem((experts, 16, part_p // 2), BF16),
+            vmem((experts, 16, part_p // 2), BF16),
+            vmem((experts, 16, (half - part_p) // 2 + LANES), BF16),
+            vmem((experts, 16, (half - part_p) // 2 + LANES), BF16),
             vmem((experts, 16, half // 2), BF16),
             vmem((experts, 16, half // 2), BF16),
             vmem((8, block, full), BF16),
@@ -624,15 +657,17 @@
             vmem((slots, 4 * units), BF16),
             vmem((slots, 2 * units), BF16),
             vmem((8, block, half), BF16),
-            vmem((4, block, part_p), BF16),
-            vmem((2, mid, part_p), BF16),
-            vmem((2, block, part_p), BF16),
-            vmem((2, 2, mid, part_q), BF16),
-            vmem((2, 2, block, part_q), BF16),
-            vmem((block, part_q), BF16),
+            vmem((4, block, sum_p), BF16),
+            vmem((2, mid, sum_p), BF16),
+            vmem((2, block, sum_p), BF16),
+            vmem((2, 2, mid, sum_q), BF16),
+            vmem((2, 2, block, sum_q), BF16),
+            vmem((block, sum_q), BF16),
             vmem((block, half), BF16),
-            vmem((experts, 16, half // 2), BF16),
-            vmem((experts, 16, half // 2), BF16),
+            vmem((experts, 16, sum_p // 2), BF16),
+            vmem((experts, 16, sum_p // 2), BF16),
+            vmem((experts, 16, sum_q // 2), BF16),
+            vmem((experts, 16, sum_q // 2), BF16),
             vmem((2, 16, half), BF16),
             vmem((2, half, 2 * units), BF16),
             vmem((2 * units, half), BF16),
@@ -640,7 +675,7 @@
             vmem((2 * units, half), BF16),
             pltpu.SemaphoreType.DMA((messages,)),
             pltpu.SemaphoreType.DMA((messages,)),
-            pltpu.SemaphoreType.DMA((16,)),
+            pltpu.SemaphoreType.DMA((24,)),
         ],
         compiler_params=pltpu.CompilerParams(
             collective_id=0,
@@ -651,9 +686,7 @@
             flops=6_000_000_000, bytes_accessed=30_000_000, transcendentals=32768
         ),
     )(
-        copy_plan,
-        assign.reshape(rows_in),
-        copy_share.reshape(experts),
+        jnp.concatenate([copy_plan, assign.reshape(rows_in), copy_share.reshape(experts)]),
         tokens,
         grad_out,
         w_gate,

time: 119 us -> 113 us (0.950)
  Pallas kernels: 114 us -> 110 us
  local copies, waits for them, and re-layouts: 3.75 us -> 1.8 us
    pallas_call x1, Pallas kernels: 110 us -> 105 us  [body(): pl.pallas_call(functools.partial(kernel, experts, half, part_p, sum_p, ch...]
    unnamed x10 -> x4, local copies, waits for them, and re-layouts: 3.75 us -> 1.8 us
where the time goes in v3:
time: 113 us
  Pallas kernels  110 us (97%)
  local copies, waits for them, and re-layouts  1.8 us (2%)
    pallas_call x1, Pallas kernels, body(): pl.pallas_call(functools.partial(kernel, experts, half, part_p, sum_p, ch...  105 us
    pallas_call x1, Pallas kernels, body(): pl.pallas_call(finish, out_shape=[jax.ShapeDtypeStruct(tokens.shape, BF16...  4.88 us

profile of v3, /device:TPU:1, one launch (start us, length us, event | category | flops | bytes accessed | tf_op | source)
XLA Modules:
  0.0 112.9 jit_solution(4435472357511345157)
XLA Ops:
  0.6 0.8 pad_add_fusion.ints_in
  1.4 0.0 copy-start
  1.4 0.9 copy-done
  2.3 0.0 copy-start.1
  2.3 0.9 copy-done.1
  3.2 104.8 %shard_map.143 = (bf16[2,16,3584]{2,1,0:T(8,128)(2,1)S(1)}, bf16[1,7168,128]{2,1,0:T(8,128)(2,1)S(1)}, bf16[1,7168,128]{2,1,0:T(8,128)(2,1)S(1)}, bf16[1,128,716...) custom-call(s32[24]{0:T(128)S(1)} %pad_add_fusion.ints_in, ...), custom_call_target="tpu_custom_call" | custom-call | flops 6000000000 | bytes 30000000 | tf_op jit(solution)/shard_map/pallas_call | solution.py:615
  108.0 4.9 %shard_map.144 = (bf16[8,7168]{1,0:T(8,128)(2,1)}, bf16[8,7168]{1,0:T(8,128)(2,1)}, bf16[1,7168,128]{2,1,0:T(8,128)(2,1)}, bf16[1,7168,128]{2,1,0:T(8,128)(2,1)}...) custom-call(bf16[2,16,3584]{2,1,0:T(8,128)(2,1)S(1)} %get-tuple-elem, ...), custom_call_target="tpu_custom_call" | custom-call | tf_op jit(solution)/shard_map/pallas_call | solution.py:696
Async XLA Ops:
  1.4 0.9 copy-start
  2.3 0.9 copy-start.1

commit v4 on v3

v4 whole, which is shorter than its diff:
```python
import functools

import jax
import jax.numpy as jnp
from jax import lax
from jax.experimental import pallas as pl
from jax.experimental.pallas import tpu as pltpu
from jax.sharding import PartitionSpec as P

MESH = pl.DeviceIdType.MESH
BF16 = jnp.bfloat16
F32 = jnp.float32
LANES = 128


def dot(a, b):
    return jnp.dot(a, b, preferred_element_type=F32)


def dot_nt(a, b):
    return lax.dot_general(a, b, (((1,), (1,)), ((), ())), preferred_element_type=F32)


def dot_tn(a, b):
    return lax.dot_general(a, b, (((0,), (0,)), ((), ())), preferred_element_type=F32)


def kernel(
    experts,
    half,
    part_p,
    sum_p,
    chunk,
    ints_in,
    rows_in,
    w_gate,
    w_up,
    w_down,
    o_out,
    gate_out,
    up_out,
    down_out,
    copy_gate_out,
    copy_up_out,
    copy_down_out,
    ints,
    rows_ref,
    lines,
    own_send_p,
    own_recv_p,
    own_send_q,
    own_recv_q,
    cpy_send,
    cpy_recv,
    own,
    cpy,
    w1,
    wd,
    pre,
    pre_recv,
    acts,
    gx1,
    gx2s,
    gx2,
    gcat,
    hcat,
    part,
    rz,
    rxo,
    rxf,
    ro_q,
    rf_q,
    rzq,
    fin,
    back_send_p,
    back_recv_p,
    back_send_q,
    back_recv_q,
    outs,
    st1,
    st2,
    ct1,
    ct2,
    ssem,
    rsem,
    lsem,
):
    units = w1.shape[2] // 2
    full = half + LANES
    per_chip = 4 * experts
    slots = 8 * per_chip
    block = 2 * per_chip
    mid = block // 2
    steps = half // chunk
    sum_q = half - sum_p

    dp = lax.axis_index("dp")
    ex = lax.axis_index("expert")
    x = dp // 4
    z = (dp // 2) % 2
    c = dp % 2
    o = 1 - c

    def chip(dx, zz):
        return lax.rem(x + dx, 4) * 2 + zz

    me = chip(0, z)
    xp = (lax.rem(dp + 4, 16), ex)
    xm = (lax.rem(dp + 12, 16), ex)
    zp = (dp + 2 - 4 * z, ex)
    sib = (dp + 1 - 2 * c, ex)

    def peer(i, other=False):
        return (sib[0] if other else dp, lax.rem(ex + i, experts))

    used = [0]
    sends = []

    def fresh():
        used[0] += 1
        return used[0] - 1

    def msg(k, src, dst, dev):
        copy = pltpu.make_async_remote_copy(
            src_ref=src,
            dst_ref=dst,
            send_sem=ssem.at[k],
            recv_sem=rsem.at[k],
            device_id=dev,
            device_id_type=MESH,
        )
        copy.start()
        sends.append(copy)

    def got(k, ref, dev):
        pltpu.make_async_remote_copy(
            src_ref=ref,
            dst_ref=ref,
            send_sem=ssem.at[k],
            recv_sem=rsem.at[k],
            device_id=dev,
            device_id_type=MESH,
        ).wait_recv()

    used_local = [0]

    def local(src, dst):
        copy = pltpu.make_async_copy(src, dst, lsem.at[used_local[0]])
        used_local[0] += 1
        copy.start()
        return copy

    my_rows = pl.ds(pl.multiple_of(c * half, half), half)
    other_rows = pl.ds(pl.multiple_of(o * half, half), half)

    first_loads = [
        local(ints_in, ints),
        local(rows_in, rows_ref),
    ]

    barrier = pltpu.get_barrier_semaphore()
    greeted = [xp, xm, zp] + [peer(i) for i in range(1, experts)]
    greeted += [peer(i, True) for i in range(experts)]
    for dev in greeted:
        pl.semaphore_signal(barrier, inc=1, device_id=dev, device_id_type=MESH)

    weight_loads = [
        local(w_gate.at[0, my_rows, :], w1.at[0, :, pl.ds(0, units)]),
        local(w_up.at[0, my_rows, :], w1.at[0, :, pl.ds(units, units)]),
        local(w_down.at[0, :, my_rows], wd.at[pl.ds(0, units), :]),
    ]

    for load in first_loads:
        load.wait()

    size = 16 * experts
    line = lax.broadcasted_iota(jnp.int32, (16, LANES), 0)
    owned = jnp.zeros((16, LANES), jnp.int32)
    copied = jnp.zeros((16, LANES), jnp.int32)
    flags = jnp.zeros((16, LANES), F32)
    named = [ints[experts + t] for t in range(8)]
    for t in range(8):
        rank = jnp.int32(0)
        for earlier in range(t):
            rank += (named[earlier] == named[t]).astype(jnp.int32)
        holder = jnp.int32(0)
        for i in range(1, experts):
            holder += i * (ints[i] == named[t]).astype(jnp.int32)
        moved = (rank < ints[experts + 8 + named[t]]).astype(jnp.int32)
        here = line % 8 == t
        owned = jnp.where(here, named[t] * 16 + rank, owned)
        copied = jnp.where(here, moved * (holder * 16 + rank) - (1 - moved) * LANES, copied)
        flags = jnp.where(here, moved.astype(F32), flags)
    lane = lax.broadcasted_iota(jnp.int32, (16, LANES), 1) - (line // 8) * 2
    own_marks = [(lane == owned + 4 * q).astype(F32).astype(BF16)[:, :size] for q in range(4)]
    cpy_marks = [(lane == copied + 4 * q).astype(F32).astype(BF16)[:, :size] for q in range(4)]
    flags = flags.astype(BF16)

    lines[...] = jnp.concatenate(
        [rows_ref[0].astype(F32), rows_ref[1].astype(F32)], axis=0
    ).astype(BF16)
    pl.semaphore_wait(barrier, len(greeted))

    def spread(marks, side, start, count):
        total = None
        for q in range(4):
            begin = side * half + start + q * (count // 4)
            term = dot_tn(marks[q], lines[:, begin : begin + count // 4])
            total = term if total is None else total + term
        return total.astype(BF16).reshape(experts, 16, count // 4)

    def exchange(source, target):
        keys = [[fresh() for _ in range(experts)] for _ in range(2)]
        for i in range(1, experts):
            dev = peer(i)
            msg(keys[0][i], source.at[c, dev[1]], target.at[c, ex], dev)
            dev = peer(i, True)
            msg(keys[1][i], source.at[o, dev[1]], target.at[c, ex], dev)
        msg(keys[1][0], source.at[o, ex], target.at[c, ex], sib)
        target[c, ex] = source[c, ex]

        def arrive():
            for i in range(experts):
                at = lax.rem(ex + experts - i, experts)
                if i > 0:
                    got(keys[0][i], target.at[c, at], peer(i))
                got(keys[1][i], target.at[o, at], peer(i, True))

        return arrive

    for side in range(2):
        own_send_p[side] = spread(own_marks, side, 0, sum_p)
    arrive_p = exchange(own_send_p, own_recv_p)
    side_q = sum_q // 4
    marked = dot_tn(own_marks[0], flags).astype(BF16).reshape(experts, 16, LANES)
    for side in range(2):
        own_send_q[side, :, :, :side_q] = spread(own_marks, side, sum_p, sum_q)
        own_send_q[side, :, :, side_q:] = marked
    arrive_q = exchange(own_send_q, own_recv_q)
    for side in range(2):
        cpy_send[side] = spread(cpy_marks, side, 0, half)
    arrive_cpy = exchange(cpy_send, cpy_recv)
    k_w = [fresh() for _ in range(3)]
    msg(k_w[0], w_gate.at[0, other_rows, :], w1.at[1, :, pl.ds(0, units)], sib)
    msg(k_w[1], w_up.at[0, other_rows, :], w1.at[1, :, pl.ds(units, units)], sib)
    msg(k_w[2], w_down.at[0, :, other_rows], wd.at[pl.ds(units, units), :], sib)

    def places(shape, out, slot):
        to = lax.broadcasted_iota(jnp.int32, shape, out)
        fr = lax.broadcasted_iota(jnp.int32, shape, slot)
        row = ((fr // 2) % 2) * per_chip + ((fr // 16) % experts) * 4 + (fr // size) * 2 + fr % 2
        same = to == row
        return [
            jnp.logical_and(same, (fr // 4) % 4 == q).astype(F32).astype(BF16) for q in range(4)
        ]

    take = places((block, 2 * size), 0, 1)

    def collect(buf, arrived, start, count):
        part = count // 4
        rows = arrived[:, :, :, :part].reshape(2 * size, part)
        for q in range(4):
            buf[me, :, start + q * part : start + (q + 1) * part] = dot(take[q], rows).astype(BF16)

    def gather(buf, width, part_p):
        keys = [fresh() for _ in range(18)]

        def cut(q, lane, row=None):
            start, count = (0, block) if row is None else (row * mid, mid)
            if lane == 0:
                return buf.at[q, pl.ds(start, count), pl.ds(0, part_p)]
            return buf.at[q, pl.ds(start, count), pl.ds(part_p, width - part_p)]

        moves = {
            0: (me, 0, None, xp),
            1: (me, 0, None, xm),
            2: (me, 0, None, zp),
            3: (chip(3, z), 0, 0, xp),
            4: (chip(1, z), 0, 1, xm),
            5: (chip(3, z), 0, None, zp),
            6: (chip(1, z), 0, None, zp),
            7: (chip(2, z), 0, 0, zp),
            8: (chip(2, z), 0, 1, zp),
            9: (me, 1, None, zp),
            10: (me, 1, None, xp),
            11: (me, 1, None, xm),
            12: (chip(0, y), 1, None, xp),
            13: (chip(0, y), 1, None, xm),
            14: (chip(3, z), 1, 0, xp),
            15: (chip(1, z), 1, 1, xm),
            16: (chip(3, y), 1, 0, xp),
            17: (chip(1, y), 1, 1, xm),
        }
        lands = {
            0: (chip(3, z), 0, None, xm),
            1: (chip(1, z), 0, None, xp),
            2: (chip(0, y), 0, None, zp),
            3: (chip(2, z), 0, 0, xm),
            4: (chip(2, z), 0, 1, xp),
            5: (chip(3, y), 0, None, zp),
            6: (chip(1, y), 0, None, zp),
            7: (chip(2, y), 0, 0, zp),
            8: (chip(2, y), 0, 1, zp),
            9: (chip(0, y), 1, None, zp),
            10: (chip(3, z), 1, None, xm),
            11: (chip(1, z), 1, None, xp),
            12: (chip(3, y), 1, None, xm),
            13: (chip(1, y), 1, None, xp),
            14: (chip(2, z), 1, 0, xm),
            15: (chip(2, z), 1, 1, xp),
            16: (chip(2, y), 1, 0, xm),
            17: (chip(2, y), 1, 1, xp),
        }
        after = {3: 0, 5: 0, 4: 1, 6: 1, 12: 9, 13: 9, 14: 10, 15: 11, 7: 3, 8: 4, 16: 12, 17: 13}
        seen = set()

        def arrive(i):
            if i not in seen:
                seen.add(i)
                q, lane, row, dev = lands[i]
                got(keys[i], cut(q, lane, row), dev)

        def go(*numbers):
            for i in numbers:
                if i in after:
                    arrive(after[i])
                q, lane, row, dev = moves[i]
                msg(keys[i], cut(q, lane, row), cut(q, lane, row), dev)

        def all_in():
            for i in sorted(lands):
                arrive(i)

        return go, all_in

    y = 1 - z
    go_own, own_in = gather(own, full, 10 * LANES)
    go_cpy, cpy_in = gather(cpy, half, 8 * LANES)
    arrive_p()
    collect(own, own_recv_p, 0, sum_p)
    go_own(0, 1)
    arrive_q()
    collect(own, own_recv_q, sum_p, sum_q)
    own[me, :, half:] = dot(
        take[0], own_recv_q[:, :, :, side_q:].reshape(2 * size, LANES)
    ).astype(BF16)

    def copy_block():
        arrive_cpy()
        collect(cpy, cpy_recv, 0, half)

    def tokens_of(buf, cols):
        return buf[:, :per_chip, cols].reshape(slots, -1)

    def backs_of(buf, cols):
        return buf[:, per_chip:, cols].reshape(slots, -1)

    k_pre = fresh()
    k_acts = fresh()
    activations = acts.at[0]
    piece_rows = slots // experts

    def gates():
        for load in weight_loads:
            load.wait()
        got(k_w[0], w1.at[1, :, pl.ds(0, units)], sib)
        got(k_w[1], w1.at[1, :, pl.ds(units, units)], sib)
        got(k_w[2], wd.at[pl.ds(units, units), :], sib)
        own_in()
        pre[1, :, : 2 * units] = dot(tokens_of(own, slice(0, half)), w1[1])
        gh = dot_nt(backs_of(own, slice(0, half)), wd[...])
        pre[1, :, 2 * units :] = gh[:, units:]
        msg(k_pre, pre.at[1], pre_recv, sib)
        pre[0, :, : 2 * units] = dot(tokens_of(own, slice(0, half)), w1[0])
        pre[0, :, 2 * units :] = gh[:, :units]

    k_gx1 = [fresh() for _ in range(experts - 1)]
    k_gx2 = [fresh() for _ in range(experts - 1)]

    def activate():
        got(k_pre, pre_recv, sib)
        total = pre[0] + pre_recv[...]
        gate = total[:, :units]
        up = total[:, units : 2 * units]
        grad_hidden = total[:, 2 * units :]
        squash = jax.nn.sigmoid(gate)
        acts[0, :, :units] = (gate * squash * up).astype(BF16)
        acts[0, :, units : 2 * units] = (
            grad_hidden * up * squash * (1.0 + gate * (1.0 - squash))
        ).astype(BF16)
        acts[0, :, 2 * units :] = (grad_hidden * gate * squash).astype(BF16)
        msg(k_acts, activations, acts.at[1], sib)
        for i in range(1, experts):
            dev = peer(i)
            piece = pl.ds(pl.multiple_of(dev[1] * piece_rows, piece_rows), piece_rows)
            msg(k_gx1[i - 1], acts.at[0, piece, :], gx1.at[ex], dev)
        piece = pl.ds(pl.multiple_of(ex * piece_rows, piece_rows), piece_rows)
        gx1[ex] = acts[0, piece, :]

    def partials():
        got(k_acts, acts.at[1], sib)
        hcat[:, :units] = acts[0, :, :units]
        hcat[:, units:] = acts[1, :, :units]

        @pl.loop(0, steps)
        def _(step):
            cols = pl.ds(pl.multiple_of(step * chunk, chunk), chunk)
            m = dot(hcat[...], wd[:, cols])
            part[:, :per_chip, cols] = m.astype(BF16).reshape(8, per_chip, chunk)
            r = dot_nt(acts[0, :, units:], w1[0, cols, :]) + dot_nt(
                acts[1, :, units:], w1[1, cols, :]
            )
            part[:, per_chip:, cols] = r.astype(BF16).reshape(8, per_chip, chunk)

    def choose():
        for i in range(1, experts):
            got(k_gx1[i - 1], gx1.at[lax.rem(ex + experts - i, experts)], peer(i))
        for i in range(experts):
            gx2s[i] = gx1[ints[i]]
        for i in range(1, experts):
            dev = peer(i)
            msg(k_gx2[i - 1], gx2s.at[dev[1]], gx2.at[0, ex], dev)
        gx2[0, ex] = gx2s[ex]

    cols_p = pl.ds(0, sum_p)
    cols_q = pl.ds(sum_p, sum_q)
    first_rows = pl.ds(0, mid)
    last_rows = pl.ds(mid, mid)
    every = pl.ds(0, block)

    k_z = [fresh() for _ in range(4)]
    k_xo = [fresh() for _ in range(2)]
    k_xf = [fresh() for _ in range(2)]
    k_yo = [[fresh() for _ in range(2)] for _ in range(2)]
    k_yf = [[fresh() for _ in range(2)] for _ in range(2)]
    k_w0 = fresh()

    def add(ref, extra):
        ref[...] = (ref[...].astype(F32) + extra[...].astype(F32)).astype(BF16)

    def send_z(*numbers):
        for j in numbers:
            msg(k_z[j], part.at[chip(j, y), every, cols_p], rz.at[j], zp)

    def send_far(i):
        zz = (y, z)[i]
        msg(k_yo[i][0], part.at[chip(2, zz), first_rows, cols_q], ro_q.at[i, 0], xp)
        msg(k_yo[i][1], part.at[chip(2, zz), last_rows, cols_q], ro_q.at[i, 1], xm)

    def keep_weights():
        copied = own[:, :per_chip, half:full].reshape(slots, LANES).astype(F32)[:, :1]
        kept = 1.0 - copied
        gcat[:, : 2 * units] = (acts[0, :, units:].astype(F32) * kept).astype(BF16)
        gcat[:, 2 * units :] = (acts[1, :, units:].astype(F32) * kept).astype(BF16)
        hcat[...] = (hcat[...].astype(F32) * kept).astype(BF16)
        weight_grads(own, st1, st2, 0, steps)

    def weight_grads(buf, one, two, begin, end):
        @pl.loop(begin, end)
        def _(step):
            cols = pl.ds(pl.multiple_of(step * chunk, chunk), chunk)
            d = dot_tn(tokens_of(buf, cols), gcat[...]).astype(BF16)
            one[0, cols, :] = d[:, : 2 * units]
            one[1, cols, :] = d[:, 2 * units :]
            two[:, cols] = dot_tn(hcat[...], backs_of(buf, cols)).astype(BF16)

    def write_grads(one, two, g_out, u_out, d_out, begin, end):
        keys = [fresh() for _ in range(3)]
        lanes_g, lanes_u = pl.ds(0, units), pl.ds(units, units)
        start, count = begin * chunk, (end - begin) * chunk
        src = pl.ds(start, count)
        to_mine = pl.ds(pl.multiple_of(c * half + start, LANES), count)
        to_other = pl.ds(pl.multiple_of(o * half + start, LANES), count)
        msg(keys[0], one.at[1, src, lanes_g], g_out.at[0, to_mine, :], sib)
        msg(keys[1], one.at[1, src, lanes_u], u_out.at[0, to_mine, :], sib)
        msg(keys[2], two.at[lanes_u, src], d_out.at[0, :, to_mine], sib)
        mine = [
            local(one.at[0, src, lanes_g], g_out.at[0, to_mine, :]),
            local(one.at[0, src, lanes_u], u_out.at[0, to_mine, :]),
            local(two.at[lanes_g, src], d_out.at[0, :, to_mine]),
        ]

        def finish():
            for copy in mine:
                copy.wait()
            got(keys[0], g_out.at[0, to_other, :], sib)
            got(keys[1], u_out.at[0, to_other, :], sib)
            got(keys[2], d_out.at[0, :, to_other], sib)

        return finish

    def pass_on(i, right):
        zz = (y, z)[i]
        if right:
            got(k_yo[i][0], ro_q.at[i, 0], xm)
            add(part.at[chip(1, zz), first_rows, cols_q], ro_q.at[i, 0])
            msg(k_yf[i][0], part.at[chip(1, zz), every, cols_q], rf_q.at[i, 0], xp)
        else:
            got(k_yo[i][1], ro_q.at[i, 1], xp)
            add(part.at[chip(3, zz), last_rows, cols_q], ro_q.at[i, 1])
            msg(k_yf[i][1], part.at[chip(3, zz), every, cols_q], rf_q.at[i, 1], xm)

    def sum_z(j):
        got(k_z[j], rz.at[j], zp)
        add(part.at[chip(j, z), every, cols_p], rz.at[j])

    def send_opposite():
        sum_z(2)
        msg(k_xo[0], part.at[chip(2, z), first_rows, cols_p], rxo.at[0], xp)
        msg(k_xo[1], part.at[chip(2, z), last_rows, cols_p], rxo.at[1], xm)

    def send_right():
        got(k_xo[0], rxo.at[0], xm)
        add(part.at[chip(1, z), first_rows, cols_p], rxo.at[0])
        msg(k_xf[0], part.at[chip(1, z), every, cols_p], rxf.at[0], xp)

    def send_left():
        got(k_xo[1], rxo.at[1], xp)
        add(part.at[chip(3, z), last_rows, cols_p], rxo.at[1])
        msg(k_xf[1], part.at[chip(3, z), every, cols_p], rxf.at[1], xm)

    def send_last():
        got(k_yf[0][0], rf_q.at[0, 0], xm)
        got(k_yf[0][1], rf_q.at[0, 1], xp)
        mine_y = part.at[chip(0, y), every, cols_q]
        mine_y[...] = (
            mine_y[...].astype(F32) + rf_q[0, 0].astype(F32) + rf_q[0, 1].astype(F32)
        ).astype(BF16)
        msg(k_w0, mine_y, rzq, zp)

    k_gsib = fresh()

    def share_choice():
        for i in range(1, experts):
            got(k_gx2[i - 1], gx2.at[0, lax.rem(ex + experts - i, experts)], peer(i))
        msg(k_gsib, gx2.at[0], gx2.at[1], sib)

    def copy_weights():
        got(k_gsib, gx2.at[1], sib)
        cpy_in()
        for i in range(2):
            gcat[:, 2 * units * i : 2 * units * (i + 1)] = gx2[i, :, :, units:].reshape(
                slots, 2 * units
            )
            hcat[:, units * i : units * (i + 1)] = gx2[i, :, :, :units].reshape(slots, units)
        weight_grads(cpy, ct1, ct2, 0, steps)

    go_own(9, 10, 11, 3, 5, 4, 6, 12, 13, 2, 14, 15, 7, 8, 16, 17)
    copy_block()
    go_cpy(0, 1, 9, 10, 11)
    gates()
    go_cpy(3, 5, 4, 6, 12, 13, 2)
    activate()
    partials()
    send_z(2, 1, 3, 0)
    send_far(0)
    send_far(1)
    go_cpy(14, 15, 7, 8, 16, 17)
    choose()
    keep_weights()
    finish_own = write_grads(st1, st2, gate_out, up_out, down_out, 0, steps)
    pass_on(0, True)
    pass_on(0, False)
    send_opposite()
    sum_z(1)
    sum_z(3)
    pass_on(1, True)
    pass_on(1, False)
    send_right()
    send_left()
    send_last()
    share_choice()
    copy_weights()
    copy_outs = (copy_gate_out, copy_up_out, copy_down_out)
    finish_cpy = write_grads(ct1, ct2, *copy_outs, 0, steps)
    put = places((2 * size, block), 1, 0)

    def pack(start, count):
        total = None
        for q in range(4):
            begin = start + q * (count // 4)
            term = dot(put[q], fin[:, begin : begin + count // 4])
            total = term if total is None else total + term
        return total.astype(BF16).reshape(2, experts, 16, count // 4)

    got(k_yf[1][0], rf_q.at[1, 0], xm)
    got(k_yf[1][1], rf_q.at[1, 1], xp)
    got(k_w0, rzq, zp)
    fin[:, cols_q] = (
        part[me, :, cols_q].astype(F32)
        + rf_q[1, 0].astype(F32)
        + rf_q[1, 1].astype(F32)
        + rzq[...].astype(F32)
    ).astype(BF16)
    back_send_q[...] = pack(sum_p, sum_q)
    back_q = exchange(back_send_q, back_recv_q)
    got(k_z[0], rz.at[0], zp)
    got(k_xf[0], rxf.at[0], xm)
    got(k_xf[1], rxf.at[1], xp)
    fin[:, cols_p] = (
        part[me, :, cols_p].astype(F32)
        + rz[0].astype(F32)
        + rxf[0].astype(F32)
        + rxf[1].astype(F32)
    ).astype(BF16)
    back_send_p[...] = pack(0, sum_p)
    back_p = exchange(back_send_p, back_recv_p)

    def restore(buf, start, count):
        part = count // 4
        for side in range(2):
            rows = buf[side].reshape(size, part)
            for q in range(4):
                begin = start + q * part
                outs[side, :, begin : begin + part] = dot(own_marks[q], rows).astype(BF16)

    back_q()
    restore(back_recv_q, sum_p, sum_q)
    back_p()
    restore(back_recv_p, 0, sum_p)
    mine_out = local(outs, o_out)
    mine_out.wait()
    finish_own()
    finish_cpy()
    for copy in sends:
        copy.wait_send()


def finish(o, g, u, d, cg, cu, cd, mixed, grad_in, g_out, u_out, d_out, cg_out, cu_out, cd_out, sem):
    copies = []
    pairs = ((g, g_out), (u, u_out), (d, d_out), (cg, cg_out), (cu, cu_out), (cd, cd_out))
    for i, (src, dst) in enumerate(pairs):
        copies.append(pltpu.make_async_copy(src, dst, sem.at[i]))
        copies[-1].start()
    half = o.shape[2]
    for side in range(2):
        mixed[:, half * side : half * (side + 1)] = o[side, :8, :]
        grad_in[:, half * side : half * (side + 1)] = o[side, 8:, :]
    for copy in copies:
        copy.wait()


def body(tokens, assign, copy_share, copy_plan, grad_out, w_gate, w_up, w_down):
    rows_in, width = tokens.shape
    experts = lax.axis_size("expert")
    units = w_gate.shape[2]
    half = width // 2
    full = half + LANES
    chunk = half // 7
    part_p = 10 * (chunk // 4)
    per_chip = 4 * experts
    slots = 8 * per_chip
    block = 2 * per_chip
    mid = block // 2
    vmem = pltpu.VMEM
    sum_p = 12 * (chunk // 4)
    sum_q = half - sum_p
    messages = 160
    any_spec = pl.BlockSpec(memory_space=pl.ANY)
    vmem_spec = pl.BlockSpec(memory_space=pltpu.VMEM)
    o, g, u, d, cg, cu, cd = pl.pallas_call(
        functools.partial(kernel, experts, half, part_p, sum_p, chunk),
        out_shape=[
            jax.ShapeDtypeStruct((2, 16, half), BF16),
            jax.ShapeDtypeStruct(w_gate.shape, BF16),
            jax.ShapeDtypeStruct(w_up.shape, BF16),
            jax.ShapeDtypeStruct(w_down.shape, BF16),
            jax.ShapeDtypeStruct(w_gate.shape, BF16),
            jax.ShapeDtypeStruct(w_up.shape, BF16),
            jax.ShapeDtypeStruct(w_down.shape, BF16),
        ],
        in_specs=[
            any_spec,
            any_spec,
            any_spec,
            any_spec,
            any_spec,
        ],
        out_specs=[any_spec] * 7,
        scratch_shapes=[
            pltpu.SMEM((2 * experts + rows_in,), jnp.int32),
            vmem((2, rows_in, width), BF16),
            vmem((16, width), BF16),
            vmem((2, experts, 16, sum_p // 4), BF16),
            vmem((2, experts, 16, sum_p // 4), BF16),
            vmem((2, experts, 16, sum_q // 4 + LANES), BF16),
            vmem((2, experts, 16, sum_q // 4 + LANES), BF16),
            vmem((2, experts, 16, half // 4), BF16),
            vmem((2, experts, 16, half // 4), BF16),
            vmem((8, block, full), BF16),
            vmem((8, block, half), BF16),
            vmem((2, half, 2 * units), BF16),
            vmem((2 * units, half), BF16),
            vmem((2, slots, 3 * units), F32),
            vmem((slots, 3 * units), F32),
            vmem((2, slots, 3 * units), BF16),
            vmem((experts, slots // experts, 3 * units), BF16),
            vmem((experts, slots // experts, 3 * units), BF16),
            vmem((2, experts, slots // experts, 3 * units), BF16),
            vmem((slots, 4 * units), BF16),
            vmem((slots, 2 * units), BF16),
            vmem((8, block, half), BF16),
            vmem((4, block, sum_p), BF16),
            vmem((2, mid, sum_p), BF16),
            vmem((2, block, sum_p), BF16),
            vmem((2, 2, mid, sum_q), BF16),
            vmem((2, 2, block, sum_q), BF16),
            vmem((block, sum_q), BF16),
            vmem((block, half), BF16),
            vmem((2, experts, 16, sum_p // 4), BF16),
            vmem((2, experts, 16, sum_p // 4), BF16),
            vmem((2, experts, 16, sum_q // 4), BF16),
            vmem((2, experts, 16, sum_q // 4), BF16),
            vmem((2, 16, half), BF16),
            vmem((2, half, 2 * units), BF16),
            vmem((2 * units, half), BF16),
            vmem((2, half, 2 * units), BF16),
            vmem((2 * units, half), BF16),
            pltpu.SemaphoreType.DMA((messages,)),
            pltpu.SemaphoreType.DMA((messages,)),
            pltpu.SemaphoreType.DMA((24,)),
        ],
        compiler_params=pltpu.CompilerParams(
            collective_id=0,
            has_side_effects=True,
            vmem_limit_bytes=42 * 1024 * 1024,
        ),
        cost_estimate=pl.CostEstimate(
            flops=6_000_000_000, bytes_accessed=30_000_000, transcendentals=32768
        ),
    )(
        jnp.concatenate([copy_plan, assign.reshape(rows_in), copy_share.reshape(experts)]),
        jnp.stack([tokens, grad_out]),
        w_gate,
        w_up,
        w_down,
    )
    return pl.pallas_call(
        finish,
        out_shape=[
            jax.ShapeDtypeStruct(tokens.shape, BF16),
            jax.ShapeDtypeStruct(tokens.shape, BF16),
            jax.ShapeDtypeStruct(w_gate.shape, BF16),
            jax.ShapeDtypeStruct(w_up.shape, BF16),
            jax.ShapeDtypeStruct(w_down.shape, BF16),
            jax.ShapeDtypeStruct(w_gate.shape, BF16),
            jax.ShapeDtypeStruct(w_up.shape, BF16),
            jax.ShapeDtypeStruct(w_down.shape, BF16),
        ],
        in_specs=[vmem_spec] + [any_spec] * 6,
        out_specs=[vmem_spec] * 2 + [any_spec] * 6,
        scratch_shapes=[pltpu.SemaphoreType.DMA((6,))],
        compiler_params=pltpu.CompilerParams(vmem_limit_bytes=4 * 1024 * 1024),
    )(o, g, u, d, cg, cu, cd)


def solution(mesh):
    placed = (
        P(("dp", "expert"), None),
        P(("dp", "expert"), None),
        P(("dp", "expert"), None),
        P(),
        P(("dp", "expert"), None),
        P("expert", None, "dp"),
        P("expert", None, "dp"),
        P("expert", "dp", None),
    )
    return jax.shard_map(
        body,
        mesh=mesh,
        in_specs=placed,
        out_specs=(
            P(("dp", "expert"), None),
            P(("dp", "expert"), None),
            P("expert", None, "dp"),
            P("expert", None, "dp"),
            P("expert", "dp", None),
            P("expert", None, "dp"),
            P("expert", None, "dp"),
            P("expert", "dp", None),
        ),
        check_vma=False,
    )
```

time: 113 us -> 110 us (0.973)
  Pallas kernels: 110 us -> 107 us
  local copies, waits for them, and re-layouts: 1.8 us -> 0 us
    pallas_call x1, Pallas kernels: 105 us -> 103 us  [body(): pl.pallas_call(functools.partial(kernel, experts, half, part_p, sum_p, ch...]
    unnamed x4 -> x0, local copies, waits for them, and re-layouts: 1.8 us -> none
where the time goes in v4:
time: 110 us
  Pallas kernels  107 us (97%)
  other arithmetic  1.74 us (2%)
    pallas_call x1, Pallas kernels, body(): pl.pallas_call(functools.partial(kernel, experts, half, part_p, sum_p, ch...  103 us
    pallas_call x1, Pallas kernels, body(): pl.pallas_call(finish, out_shape=[jax.ShapeDtypeStruct(tokens.shape, BF16...  4.88 us

profile of v4, /device:TPU:1, one launch (start us, length us, event | category | flops | bytes accessed | tf_op | source)
XLA Modules:
  0.0 109.9 jit_solution(5966981854133049451)
XLA Ops:
  0.6 0.8 pad_add_fusion.ints_in
  1.4 1.0 pad_maximum_fusion.rows_in
  2.4 102.6 %shard_map.143 = (bf16[2,16,3584]{2,1,0:T(8,128)(2,1)S(1)}, bf16[1,7168,128]{2,1,0:T(8,128)(2,1)S(1)}, bf16[1,7168,128]{2,1,0:T(8,128)(2,1)S(1)}, bf16[1,128,716...) custom-call(s32[24]{0:T(128)S(1)} %pad_add_fusion.ints_in, ...), custom_call_target="tpu_custom_call" | custom-call | flops 6000000000 | bytes 30000000 | tf_op jit(solution)/shard_map/pallas_call | solution.py:661
  105.0 4.9 %shard_map.144 = (bf16[8,7168]{1,0:T(8,128)(2,1)}, bf16[8,7168]{1,0:T(8,128)(2,1)}, bf16[1,7168,128]{2,1,0:T(8,128)(2,1)}, bf16[1,7168,128]{2,1,0:T(8,128)(2,1)}...) custom-call(bf16[2,16,3584]{2,1,0:T(8,128)(2,1)S(1)} %get-tuple-elem, ...), custom_call_target="tpu_custom_call" | custom-call | tf_op jit(solution)/shard_map/pallas_call | solution.py:738

commit v5 on v4

--- a/solution.py
+++ b/solution.py
@@ -176,7 +176,7 @@
     size = 16 * experts
     line = lax.broadcasted_iota(jnp.int32, (16, LANES), 0)
     owned = jnp.zeros((16, LANES), jnp.int32)
-    copied = jnp.zeros((16, LANES), jnp.int32)
+    targets = []
     flags = jnp.zeros((16, LANES), F32)
     named = [ints[experts + t] for t in range(8)]
     for t in range(8):
@@ -188,24 +188,36 @@
             holder += i * (ints[i] == named[t]).astype(jnp.int32)
         moved = (rank < ints[experts + 8 + named[t]]).astype(jnp.int32)
         here = line % 8 == t
-        owned = jnp.where(here, named[t] * 16 + rank, owned)
-        copied = jnp.where(here, moved * (holder * 16 + rank) - (1 - moved) * LANES, copied)
+        targets.append(
+            (named[t] * 16 + rank, moved * (holder * 16 + rank) - (1 - moved) * LANES)
+        )
+        owned = jnp.where(here, targets[t][0], owned)
         flags = jnp.where(here, moved.astype(F32), flags)
     lane = lax.broadcasted_iota(jnp.int32, (16, LANES), 1) - (line // 8) * 2
+    cast = (size, 16)
+    spot = lax.broadcasted_iota(jnp.int32, cast, 0)
+    row = lax.broadcasted_iota(jnp.int32, cast, 1)
+    owned_t = jnp.zeros(cast, jnp.int32)
+    copied_t = jnp.zeros(cast, jnp.int32)
+    for t in range(8):
+        here = row % 8 == t
+        owned_t = jnp.where(here, targets[t][0], owned_t)
+        copied_t = jnp.where(here, targets[t][1], copied_t)
+    spot = spot - (row // 8) * 2
+    own_places = [(spot == owned_t + 4 * q).astype(F32).astype(BF16) for q in range(4)]
+    cpy_places = [(spot == copied_t + 4 * q).astype(F32).astype(BF16) for q in range(4)]
     own_marks = [(lane == owned + 4 * q).astype(F32).astype(BF16)[:, :size] for q in range(4)]
-    cpy_marks = [(lane == copied + 4 * q).astype(F32).astype(BF16)[:, :size] for q in range(4)]
     flags = flags.astype(BF16)
 
     lines[...] = jnp.concatenate(
         [rows_ref[0].astype(F32), rows_ref[1].astype(F32)], axis=0
     ).astype(BF16)
-    pl.semaphore_wait(barrier, len(greeted))
 
     def spread(marks, side, start, count):
         total = None
         for q in range(4):
             begin = side * half + start + q * (count // 4)
-            term = dot_tn(marks[q], lines[:, begin : begin + count // 4])
+            term = dot(marks[q], lines[:, begin : begin + count // 4])
             total = term if total is None else total + term
         return total.astype(BF16).reshape(experts, 16, count // 4)
 
@@ -229,16 +241,17 @@
         return arrive
 
     for side in range(2):
-        own_send_p[side] = spread(own_marks, side, 0, sum_p)
+        own_send_p[side] = spread(own_places, side, 0, sum_p)
+    pl.semaphore_wait(barrier, len(greeted))
     arrive_p = exchange(own_send_p, own_recv_p)
     side_q = sum_q // 4
-    marked = dot_tn(own_marks[0], flags).astype(BF16).reshape(experts, 16, LANES)
+    marked = dot(own_places[0], flags).astype(BF16).reshape(experts, 16, LANES)
     for side in range(2):
-        own_send_q[side, :, :, :side_q] = spread(own_marks, side, sum_p, sum_q)
+        own_send_q[side, :, :, :side_q] = spread(own_places, side, sum_p, sum_q)
         own_send_q[side, :, :, side_q:] = marked
     arrive_q = exchange(own_send_q, own_recv_q)
     for side in range(2):
-        cpy_send[side] = spread(cpy_marks, side, 0, half)
+        cpy_send[side] = spread(cpy_places, side, 0, half)
     arrive_cpy = exchange(cpy_send, cpy_recv)
     k_w = [fresh() for _ in range(3)]
     msg(k_w[0], w_gate.at[0, other_rows, :], w1.at[1, :, pl.ds(0, units)], sib)
@@ -549,18 +562,18 @@
     copy_block()
     go_cpy(0, 1, 9, 10, 11)
     gates()
-    go_cpy(3, 5, 4, 6, 12, 13, 2)
     activate()
+    go_cpy(3, 5, 4, 6, 12, 13, 2, 14, 15, 7, 8)
     partials()
     send_z(2, 1, 3, 0)
     send_far(0)
     send_far(1)
-    go_cpy(14, 15, 7, 8, 16, 17)
+    pass_on(0, True)
+    pass_on(0, False)
+    go_cpy(16, 17)
     choose()
     keep_weights()
     finish_own = write_grads(st1, st2, gate_out, up_out, down_out, 0, steps)
-    pass_on(0, True)
-    pass_on(0, False)
     send_opposite()
     sum_z(1)
     sum_z(3)
@@ -573,6 +586,7 @@
     copy_weights()
     copy_outs = (copy_gate_out, copy_up_out, copy_down_out)
     finish_cpy = write_grads(ct1, ct2, *copy_outs, 0, steps)
+
     put = places((2 * size, block), 1, 0)
 
     def pack(start, count):

time: 110 us -> 110 us (level)
  no operation moved by 1% of the time
where the time goes in v5:
time: 110 us; the launch traced here: 109 us
  Pallas kernels  107 us (97%)
  other arithmetic  1.74 us (2%)
    pallas_call x1, Pallas kernels, body(): pl.pallas_call(functools.partial(kernel, experts, half, part_p, sum_p, ch...  102 us
    pallas_call x1, Pallas kernels, body(): pl.pallas_call(finish, out_shape=[jax.ShapeDtypeStruct(tokens.shape, BF16...  4.88 us

profile of v5, /device:TPU:1, one launch (start us, length us, event | category | flops | bytes accessed | tf_op | source)
XLA Modules:
  0.0 109.4 jit_solution(12350518371528959262)
XLA Ops:
  0.6 0.8 pad_add_fusion.ints_in
  1.4 1.0 pad_maximum_fusion.rows_in
  2.4 102.2 %shard_map.143 = (bf16[2,16,3584]{2,1,0:T(8,128)(2,1)S(1)}, bf16[1,7168,128]{2,1,0:T(8,128)(2,1)S(1)}, bf16[1,7168,128]{2,1,0:T(8,128)(2,1)S(1)}, bf16[1,128,716...) custom-call(s32[24]{0:T(128)S(1)} %pad_add_fusion.ints_in, ...), custom_call_target="tpu_custom_call" | custom-call | flops 6000000000 | bytes 30000000 | tf_op jit(solution)/shard_map/pallas_call | solution.py:675
  104.5 4.9 %shard_map.144 = (bf16[8,7168]{1,0:T(8,128)(2,1)}, bf16[8,7168]{1,0:T(8,128)(2,1)}, bf16[1,7168,128]{2,1,0:T(8,128)(2,1)}, bf16[1,7168,128]{2,1,0:T(8,128)(2,1)}...) custom-call(bf16[2,16,3584]{2,1,0:T(8,128)(2,1)S(1)} %get-tuple-elem, ...), custom_call_target="tpu_custom_call" | custom-call | tf_op jit(solution)/shard_map/pallas_call | solution.py:752
